TPU v7x, 32 devices: a whole 2x2x4 slice. The times are simulated.
32 devices in a mesh: band: 16 (over z, y, x), sub: 2 (over core).
Axes of the slice: x: 2, y: 2, z: 4, core: 2. Of those that a mesh axis runs over, the one named last changes fastest.
Arguments:
- node_state: bfloat16 [16384, 512], P(('band', 'sub')), may hold values from -6 to 6
- edge_state: bfloat16 [262144, 512], P(('band', 'sub')), may hold values from -6 to 6
- send_rows: int32 [32, 32, 8], P(('band', 'sub')), may hold values from 0 to 511, as said below
- edge_sender: int32 [262144], P(('band', 'sub')), may hold values from 0 to 255, as said below
- edge_receiver: int32 [262144], P(('band', 'sub')), may hold values from 0 to 511
- edge_count: int32 [32], P(('band', 'sub')), may hold values from 1 to 8192, 163840 in all
- edge_w1: bfloat16 [1536, 512], P(('band', 'sub')), may hold values from -0.15625 to 0.15625
- edge_b1: bfloat16 [512], P(('band', 'sub')), may hold values from -3 to 3
- edge_w2: bfloat16 [512, 512], P(('band', 'sub')), may hold values from -0.25 to 0.25
- edge_gain: bfloat16 [512], P(('band', 'sub')), may hold values from 0.099609375 to 1.8984375
- edge_shift: bfloat16 [512], P(('band', 'sub')), may hold values from -2 to 2
- node_w1: bfloat16 [1024, 512], P(('band', 'sub')), may hold values from -0.1875 to 0.1875
- node_b1: bfloat16 [512], P(('band', 'sub')), may hold values from -3 to 3
- node_w2: bfloat16 [512, 512], P(('band', 'sub')), may hold values from -0.25 to 0.25
- node_gain: bfloat16 [512], P(('band', 'sub')), may hold values from 0.099609375 to 1.8984375
- node_shift: bfloat16 [512], P(('band', 'sub')), may hold values from -2 to 2
- node_cot: bfloat16 [16384, 512], P(('band', 'sub')), may hold values from -6 to 6
- edge_cot: bfloat16 [262144, 512], P(('band', 'sub')), may hold values from -6 to 6
Outputs:
- node_out: bfloat16 [16384, 512], P(('band', 'sub'))
- edge_out: bfloat16 [262144, 512], P(('band', 'sub'))
- node_grad: float32 [16384, 512], P(('band', 'sub'))
- edge_grad: float32 [262144, 512], P(('band', 'sub'))
- grad_edge_w1: float32 [1536, 512], P(('band', 'sub'))
- grad_edge_b1: float32 [512], P(('band', 'sub'))
- grad_edge_w2: float32 [512, 512], P(('band', 'sub'))
- grad_edge_gain: float32 [512], P(('band', 'sub'))
- grad_edge_shift: float32 [512], P(('band', 'sub'))
- grad_node_w1: float32 [1024, 512], P(('band', 'sub'))
- grad_node_b1: float32 [512], P(('band', 'sub'))
- grad_node_w2: float32 [512, 512], P(('band', 'sub'))
- grad_node_gain: float32 [512], P(('band', 'sub'))
- grad_node_shift: float32 [512], P(('band', 'sub'))
Inputs may be any that keep to these rules, and one draw needn't show every extreme that they name: `send_rows`: each pair of devices (q, r) has a count of live slots, at most 8, exactly 8 where q and r lie in the same or adjacent bands, often none for distant bands; slots at or past the count are padding and hold 0. `edge_sender`: every edge reads a live slot of its pair. `edge_count`: edge slots of a device at or past its count are padding.
All inputs are finite; a program needn't handle non-finite values.
Results may differ from a plain program's by a relative error of at most 0.0076.
Values may be sent and summed in bfloat16 or wider, within the bound.
A program may use at most 192 MiB of HBM per device.

v0:
```python
import jax
import jax.numpy as jnp
from jax import lax
from jax.sharding import PartitionSpec as P

EPSILON = 1e-05


def layer_norm(values):
    center = values - jnp.mean(values, axis=1, keepdims=True)
    scale_inv = lax.rsqrt(jnp.mean(center * center, axis=1, keepdims=True) + EPSILON)
    return (center * scale_inv, scale_inv)


def norm_back(upstream, normed, scale_inv):
    first_mean = jnp.mean(upstream, axis=1, keepdims=True)
    second_mean = jnp.mean(upstream * normed, axis=1, keepdims=True)
    return scale_inv * (upstream - first_mean - normed * second_mean)


def silu_slope(values):
    sigma = jax.nn.sigmoid(values)
    return sigma * (1.0 + values * (1.0 - sigma))


def local(
    node_state,
    edge_state,
    send_rows,
    edge_sender,
    edge_receiver,
    edge_count,
    edge_w1,
    edge_b1,
    edge_w2,
    edge_gain,
    edge_shift,
    node_w1,
    node_b1,
    node_w2,
    node_gain,
    node_shift,
    node_cot,
    edge_cot,
):
    flt = jnp.float32
    half = jnp.bfloat16
    (
        full_ew1,
        full_eb1,
        full_ew2,
        full_egain,
        full_eshift,
        full_nw1,
        full_nb1,
        full_nw2,
        full_ngain,
        full_nshift,
    ) = (
        lax.all_gather(edge_w1, ("band", "sub"), axis=0, tiled=True),
        lax.all_gather(edge_b1, ("band", "sub"), axis=0, tiled=True),
        lax.all_gather(edge_w2, ("band", "sub"), axis=0, tiled=True),
        lax.all_gather(edge_gain, ("band", "sub"), axis=0, tiled=True),
        lax.all_gather(edge_shift, ("band", "sub"), axis=0, tiled=True),
        lax.all_gather(node_w1, ("band", "sub"), axis=0, tiled=True),
        lax.all_gather(node_b1, ("band", "sub"), axis=0, tiled=True),
        lax.all_gather(node_w2, ("band", "sub"), axis=0, tiled=True),
        lax.all_gather(node_gain, ("band", "sub"), axis=0, tiled=True),
        lax.all_gather(node_shift, ("band", "sub"), axis=0, tiled=True),
    )
    edge_bias = full_eb1.astype(flt)
    egain_f = full_egain.astype(flt)
    eshift_f = full_eshift.astype(flt)
    node_bias = full_nb1.astype(flt)
    ngain_f = full_ngain.astype(flt)
    nshift_f = full_nshift.astype(flt)
    width = node_state.shape[1]
    node_rows = node_state.shape[0]
    edge_rows = edge_state.shape[0]
    peers = send_rows.shape[1]
    slot_rows = send_rows.shape[2]
    selected = send_rows[0].reshape(peers * slot_rows)
    outgoing = jnp.take(node_state, selected, axis=0).reshape(peers, slot_rows, width)
    incoming = lax.all_to_all(outgoing, ("band", "sub"), split_axis=0, concat_axis=0, tiled=True)
    senders_all = incoming.reshape(peers * slot_rows, width)
    block_rows = min(512, edge_rows)
    live_count = edge_count[0]
    block_total = (live_count + block_rows - 1) // block_rows

    def edge_front(first_row):
        own = lax.dynamic_slice_in_dim(edge_state, first_row, block_rows, 0)
        sender_ids = lax.dynamic_slice_in_dim(edge_sender, first_row, block_rows, 0)
        receiver_ids = lax.dynamic_slice_in_dim(edge_receiver, first_row, block_rows, 0)
        joined = jnp.concatenate(
            [
                own,
                jnp.take(senders_all, sender_ids, axis=0),
                jnp.take(node_state, receiver_ids, axis=0),
            ],
            axis=1,
        )
        preact = jnp.dot(joined, full_ew1, preferred_element_type=flt) + edge_bias
        hidden = jax.nn.silu(preact).astype(half)
        projected = jnp.dot(hidden, full_ew2, preferred_element_type=flt)
        normed, scale_inv = layer_norm(projected)
        live = (first_row + jnp.arange(block_rows, dtype=jnp.int32) < live_count).astype(flt)[
            :, None
        ]
        return (own, sender_ids, receiver_ids, joined, preact, hidden, normed, scale_inv, live)

    def forward_step(step, running):
        out_rows, gathered = running
        first_row = step * block_rows
        own, sender_ids, receiver_ids, joined, preact, hidden, normed, scale_inv, live = edge_front(
            first_row
        )
        message = live * (normed * egain_f + eshift_f)
        out_rows = lax.dynamic_update_slice_in_dim(
            out_rows, (own.astype(flt) + message).astype(half), first_row, 0
        )
        gathered = gathered + jax.ops.segment_sum(message, receiver_ids, num_segments=node_rows)
        return (out_rows, gathered)

    edge_out, gathered = lax.fori_loop(
        0, block_total, forward_step, (edge_state, jnp.zeros((node_rows, width), flt))
    )
    node_joined = jnp.concatenate([node_state, gathered.astype(half)], axis=1)
    node_pre = jnp.dot(node_joined, full_nw1, preferred_element_type=flt) + node_bias
    node_hidden = jax.nn.silu(node_pre).astype(half)
    node_proj = jnp.dot(node_hidden, full_nw2, preferred_element_type=flt)
    node_normed, node_scale = layer_norm(node_proj)
    node_out = (node_state.astype(flt) + node_normed * ngain_f + nshift_f).astype(half)
    upstream = node_cot.astype(flt)
    grad_ngain = jnp.sum(upstream * node_normed, axis=0)
    grad_nshift = jnp.sum(upstream, axis=0)
    node_dproj = norm_back(upstream * ngain_f, node_normed, node_scale).astype(half)
    grad_nw2 = jnp.dot(node_hidden.T, node_dproj, preferred_element_type=flt)
    node_dpre = (
        jnp.dot(node_dproj, full_nw2.T, preferred_element_type=flt) * silu_slope(node_pre)
    ).astype(half)
    grad_nw1 = jnp.dot(node_joined.T, node_dpre, preferred_element_type=flt)
    grad_nb1 = jnp.sum(node_dpre.astype(flt), axis=0)
    node_djoined = jnp.dot(node_dpre, full_nw1.T, preferred_element_type=flt)
    node_grad = upstream + node_djoined[:, :width]
    dgathered = node_djoined[:, width:]

    def backward_step(step, running):
        grad_rows, sender_grad, node_acc, grad_w1, grad_b1, grad_w2, grad_gain, grad_shift = running
        first_row = step * block_rows
        own, sender_ids, receiver_ids, joined, preact, hidden, normed, scale_inv, live = edge_front(
            first_row
        )
        cot_rows = lax.dynamic_slice_in_dim(edge_cot, first_row, block_rows, 0).astype(flt)
        dmessage = live * (cot_rows + jnp.take(dgathered, receiver_ids, axis=0))
        grad_gain = grad_gain + jnp.sum(dmessage * normed, axis=0)
        grad_shift = grad_shift + jnp.sum(dmessage, axis=0)
        dproj = norm_back(dmessage * egain_f, normed, scale_inv).astype(half)
        grad_w2 = grad_w2 + jnp.dot(hidden.T, dproj, preferred_element_type=flt)
        dpre = (jnp.dot(dproj, full_ew2.T, preferred_element_type=flt) * silu_slope(preact)).astype(
            half
        )
        grad_w1 = grad_w1 + jnp.dot(joined.T, dpre, preferred_element_type=flt)
        grad_b1 = grad_b1 + jnp.sum(dpre.astype(flt), axis=0)
        djoined = jnp.dot(dpre, full_ew1.T, preferred_element_type=flt)
        grad_rows = lax.dynamic_update_slice_in_dim(
            grad_rows, cot_rows + djoined[:, :width], first_row, 0
        )
        sender_grad = sender_grad + jax.ops.segment_sum(
            djoined[:, width : 2 * width], sender_ids, num_segments=peers * slot_rows
        )
        node_acc = node_acc + jax.ops.segment_sum(
            djoined[:, 2 * width :], receiver_ids, num_segments=node_rows
        )
        return (grad_rows, sender_grad, node_acc, grad_w1, grad_b1, grad_w2, grad_gain, grad_shift)

    start_state = (
        edge_cot.astype(flt),
        jnp.zeros((peers * slot_rows, width), flt),
        node_grad,
        jnp.zeros(full_ew1.shape, flt),
        jnp.zeros((width,), flt),
        jnp.zeros(full_ew2.shape, flt),
        jnp.zeros((width,), flt),
        jnp.zeros((width,), flt),
    )
    edge_grad, sender_grad, node_grad, grad_ew1, grad_eb1, grad_ew2, grad_egain, grad_eshift = (
        lax.fori_loop(0, block_total, backward_step, start_state)
    )
    returned = sender_grad.reshape(peers, slot_rows, width)
    arrived = lax.all_to_all(
        returned.astype(jnp.bfloat16), ("band", "sub"), split_axis=0, concat_axis=0, tiled=True
    ).astype(returned.dtype)
    node_grad = node_grad + jax.ops.segment_sum(
        arrived.reshape(peers * slot_rows, width), selected, num_segments=node_rows
    )
    summed = (
        lax.psum_scatter(grad_ew1, ("band", "sub"), scatter_dimension=0, tiled=True),
        lax.psum_scatter(grad_eb1, ("band", "sub"), scatter_dimension=0, tiled=True),
        lax.psum_scatter(grad_ew2, ("band", "sub"), scatter_dimension=0, tiled=True),
        lax.psum_scatter(grad_egain, ("band", "sub"), scatter_dimension=0, tiled=True),
        lax.psum_scatter(grad_eshift, ("band", "sub"), scatter_dimension=0, tiled=True),
        lax.psum_scatter(grad_nw1, ("band", "sub"), scatter_dimension=0, tiled=True),
        lax.psum_scatter(grad_nb1, ("band", "sub"), scatter_dimension=0, tiled=True),
        lax.psum_scatter(grad_nw2, ("band", "sub"), scatter_dimension=0, tiled=True),
        lax.psum_scatter(grad_ngain, ("band", "sub"), scatter_dimension=0, tiled=True),
        lax.psum_scatter(grad_nshift, ("band", "sub"), scatter_dimension=0, tiled=True),
    )
    return (
        node_out,
        edge_out,
        node_grad,
        edge_grad,
        summed[0],
        summed[1],
        summed[2],
        summed[3],
        summed[4],
        summed[5],
        summed[6],
        summed[7],
        summed[8],
        summed[9],
    )


def solution(mesh):
    in_specs = (
        P(("band", "sub"), None),
        P(("band", "sub"), None),
        P(("band", "sub"), None, None),
        P(("band", "sub")),
        P(("band", "sub")),
        P(("band", "sub")),
        P(("band", "sub"), None),
        P(("band", "sub")),
        P(("band", "sub"), None),
        P(("band", "sub")),
        P(("band", "sub")),
        P(("band", "sub"), None),
        P(("band", "sub")),
        P(("band", "sub"), None),
        P(("band", "sub")),
        P(("band", "sub")),
        P(("band", "sub"), None),
        P(("band", "sub"), None),
    )
    out_specs = (
        P(("band", "sub"), None),
        P(("band", "sub"), None),
        P(("band", "sub"), None),
        P(("band", "sub"), None),
        P(("band", "sub"), None),
        P(("band", "sub")),
        P(("band", "sub"), None),
        P(("band", "sub")),
        P(("band", "sub")),
        P(("band", "sub"), None),
        P(("band", "sub")),
        P(("band", "sub"), None),
        P(("band", "sub")),
        P(("band", "sub")),
    )
    return jax.shard_map(local, mesh=mesh, in_specs=in_specs, out_specs=out_specs, check_vma=False)
```

profile of v0, /device:TPU:0, one launch (start us, length us, event | category | flops | bytes accessed | tf_op | source)
XLA Modules:
  0.0 1622.2 jit_solution(7557400288175369881)
XLA Ops:
  12.8 7.3 all-to-all-start
  24.1 40.9 %all-reduce.13 = (bf16[512]{0:T(512)(128)(2,1)S(1)}, bf16[512]{0:T(512)(128)(2,1)S(1)}, bf16[512]{0:T(512)(128)(2,1)S(1)}, bf16[512]{0:T(512)(128)(2,1)S(1)}, bf...) all-reduce(bf16[512]{0:T(512)(128)(2,1)S(1)} %dynamic-update-slice,, ...), channel_id=1, replica_groups=mesh['band'=16,'sub'=2] {'band','sub'}, use_global_device_ids=true, to_apply=%add | all-reduce | flops 3072 | bytes 12288
  66.0 11.9 copy.77
  77.9 7.4 copy.117
  85.3 11.3 convert_element_type.100
  96.6 44.2 %all_gather.32 = bf16[512,512]{1,0:T(8,128)(2,1)} all-gather(bf16[16,512]{1,0:T(8,128)(2,1)S(1)} %copy-done.24), channel_id=1, replica_groups=mesh['band'=16,'sub'=2] {'band','sub'}, dimensions={0}, use_global_device_ids=true | all-gather | bytes 540672 | tf_op jit(solution)/shard_map/all_gather | solution.py:62
  140.8 40.7 %all_gather.37 = bf16[512,512]{1,0:T(8,128)(2,1)} all-gather(bf16[16,512]{1,0:T(8,128)(2,1)S(1)} %copy-done.25), channel_id=1, replica_groups=mesh['band'=16,'sub'=2] {'band','sub'}, dimensions={0}, use_global_device_ids=true | all-gather | bytes 540672 | tf_op jit(solution)/shard_map/all_gather | solution.py:67
  181.7 179.9 %while.36 = (s32[]{:T(128)}, bf16[8192,512]{1,0:T(8,128)(2,1)}, f32[512,512]{1,0:T(8,128)S(1)}, s32[]{:T(128)}, bf16[8192,512]{1,0:T(8,128)(2,1)}, /*index=5*/s3...) while((s32[]{:T(128)}, bf16[8192,512]{1,0:T(8,128)(2,1)}, ...), condition=%wide.region_4.7_spmd, body=%wide.region_0.6_spmd.sunk | while | flops 1083977216 | bytes 24703220 | solution.py:124
  385.1 339.3 %while.37 = (s32[]{:T(128)}, f32[8192,512]{0,1:T(8,128)}, f32[256,512]{1,0:T(8,128)}, f32[512,512]{1,0:T(8,128)}, f32[1536,512]{1,0:T(8,128)}, /*index=5*/f32[51...) while((s32[]{:T(128)}, f32[8192,512]{0,1:T(8,128)}, ...), condition=%wide.region_19.22_spmd, body=%wide.region_9.21_spmd.sunk | while | flops 3245618176 | bytes 109687952 | solution.py:187
  417.0 6.7 scatter_custom_fusion.16
  459.4 6.7 scatter_custom_fusion.16
  501.7 6.7 scatter_custom_fusion.16
  544.1 6.7 scatter_custom_fusion.16
  586.5 6.7 scatter_custom_fusion.16
  628.9 6.7 scatter_custom_fusion.16
  666.7 4.6 scatter_custom_fusion.15
  671.3 6.7 scatter_custom_fusion.16
  713.7 6.7 scatter_custom_fusion.16
  729.6 520.4 %all-to-all-start.1 = ((bf16[32,8,512]{2,1,0:T(8,128)(2,1)}), bf16[32,8,512]{2,1,0:T(8,128)(2,1)S(1)}, u32[]{:S(2)}, u32[]{:S(2)}) async-start(bf16[32,8,512]{2,1,0:T(8,128)(2,1)} %convert_bitcast_fusion), calls=%async_computation.1 | async-start | bytes 524288 | tf_op jit(solution)/shard_map/all_to_all | solution.py:190
  1251.1 40.8 %all-reduce.12 = (f32[512]{0:T(512)S(1)}, f32[512]{0:T(512)S(1)}, f32[512]{0:T(512)S(1)}, f32[512]{0:T(512)S(1)}, f32[512]{0:T(512)S(1)}, /*index=5*/f32[512]{0:T(512)S(1)}) all-reduce(f32[512]{0:T(512)S(1)} %get-tuple-element.221, f32[512]{0:T(512)S(1)} %get-tuple-element.223, ...), channel_id=3, replica_groups=mesh['band'=16,'sub'=2] {'band','sub'}, use_global_device_ids=true, to_apply=%region_22.25.clone | all-reduce | flops 3072 | bytes 24576
  1295.4 17.6 %copy.85 = f32[8192,512]{1,0:T(8,128)} copy(f32[8192,512]{0,1:T(8,128)} %get-tuple-element.367) | data formatting | bytes 33554432
  1315.6 60.1 %reduce-scatter.7.cloned.1.call-done = f32[16,512]{1,0:T(8,128)} async-done(((f32[512,512]{1,0:T(8,128)}), f32[16,512]{1,0:T(8,128)}) %reduce-scatter.7.cloned.1.call-update) | async-done | bytes 32784 | tf_op jit(solution)/shard_map/reduce_scatter | solution.py:199
  1375.8 135.3 %reduce-scatter.9.cloned.1.call-done = f32[32,512]{1,0:T(8,128)} async-done(((f32[1024,512]{1,0:T(8,128)}), f32[32,512]{1,0:T(8,128)}) %reduce-scatter.9.cloned.1.call-update) | async-done | bytes 65552 | tf_op jit(solution)/shard_map/reduce_scatter | solution.py:202
  1511.0 104.1 %reduce-scatter.5.cloned.1.call-done = f32[48,512]{1,0:T(8,128)} async-done(((f32[1536,512]{1,0:T(8,128)}), f32[48,512]{1,0:T(8,128)}) %reduce-scatter.5.cloned.1.call-update) | async-done | bytes 98320 | tf_op jit(solution)/shard_map/reduce_scatter | solution.py:197
  (736 shorter events, 504.2 us)
Async XLA Ops:
  7.2 14.4 copy-start
  7.2 15.4 copy-start.26
  7.2 15.6 copy-start.27
  7.2 15.9 copy-start.28
  7.2 16.1 copy-start.29
  7.2 16.4 %copy-start.30 = (bf16[16]{0:T(256)(128)(2,1)S(1)}, bf16[16]{0:T(256)(128)(2,1)}, u32[]{:S(2)}) copy-start(bf16[16]{0:T(256)(128)(2,1)} %param.33) | copy-start | bytes 100
  7.2 16.6 %copy-start.31 = (bf16[16]{0:T(256)(128)(2,1)S(1)}, bf16[16]{0:T(256)(128)(2,1)}, u32[]{:S(2)}) copy-start(bf16[16]{0:T(256)(128)(2,1)} %param.40) | copy-start | bytes 100
  7.3 57.8 %copy-start.20 = (bf16[512,512]{1,0:T(8,128)(2,1)S(1)}, bf16[512,512]{1,0:T(8,128)(2,1)}, u32[]{:S(2)}) copy-start(bf16[512,512]{1,0:T(8,128)(2,1)} %param.42) | copy-start | bytes 1572868
  7.3 174.3 %all-gather.3.cloned.1.call-start = ((), (), s32[]{:S(2)}) async-start(), calls=%async_computation.6 | async-start | bytes 1622016 | tf_op jit(solution)/shard_map/all_gather | solution.py:60
  12.8 168.7 %all-to-all-start = ((bf16[32,8,512]{2,1,0:T(8,128)(2,1)}), bf16[32,8,512]{2,1,0:T(8,128)(2,1)S(1)}, u32[]{:S(2)}, u32[]{:S(2)}) async-start(bf16[32,8,512]{2,1,0:T(8,128)(2,1)} %bitcast_select_fusion), calls=%async_computation | async-start | bytes 524288 | tf_op jit(solution)/shard_map/all_to_all | solution.py:84
  20.1 341.5 %all-gather.5.cloned.1.call-start = ((), (), s32[]{:S(2)}) async-start(), calls=%async_computation.7 | async-start | bytes 1081344 | tf_op jit(solution)/shard_map/all_gather | solution.py:65
  20.9 1294.7 %reduce-scatter.11.cloned.1.call-start = ((), (), s32[]{:S(2)}) async-start(), calls=%async_computation.11 | async-start | bytes 1081344 | tf_op jit(solution)/shard_map/reduce_scatter | solution.py:204
  85.3 55.5 %copy-start.25 = (bf16[16,512]{1,0:T(8,128)(2,1)S(1)}, bf16[16,512]{1,0:T(8,128)(2,1)}, u32[]{:S(2)}) copy-start(bf16[16,512]{1,0:T(8,128)(2,1)} %param.39) | copy-start | bytes 49156
  371.8 1003.9 %reduce-scatter.7.cloned.1.call-start = ((), (), s32[]{:S(2)}) async-start(), calls=%async_computation.9 | async-start | bytes 1081344 | tf_op jit(solution)/shard_map/reduce_scatter | solution.py:199
  581.9 11.3 slice-start
  624.3 11.3 slice-start
  666.7 11.3 slice-start
  724.4 786.6 %reduce-scatter.9.cloned.1.call-start = ((), (), s32[]{:S(2)}) async-start(), calls=%async_computation.10 | async-start | bytes 2162688 | tf_op jit(solution)/shard_map/reduce_scatter | solution.py:202
  727.8 522.2 %copy-start.23 = (s32[1,32,8]{2,1,0:T(8,128)S(1)}, s32[1,32,8]{2,1,0:T(8,128)}, u32[]{:S(2)}) copy-start(s32[1,32,8]{2,1,0:T(8,128)} %copy-done.22) | copy-start | bytes 3076
  727.8 522.3 %copy-start.14 = (bf16[512,512]{0,1:T(8,128)(2,1)S(1)}, bf16[512,512]{0,1:T(8,128)(2,1)}, u32[]{:S(2)}) copy-start(bf16[512,512]{0,1:T(8,128)(2,1)} %get-tuple-element.496) | copy-start | bytes 1572868
  727.8 887.4 %reduce-scatter.5.cloned.1.call-start = ((), (), s32[]{:S(2)}) async-start(), calls=%async_computation.8 | async-start | bytes 3244032 | tf_op jit(solution)/shard_map/reduce_scatter | solution.py:197
  729.6 583.4 %all-to-all-start.1 = ((bf16[32,8,512]{2,1,0:T(8,128)(2,1)}), bf16[32,8,512]{2,1,0:T(8,128)(2,1)S(1)}, u32[]{:S(2)}, u32[]{:S(2)}) async-start(bf16[32,8,512]{2,1,0:T(8,128)(2,1)} %convert_bitcast_fusion), calls=%async_computation.1 | async-start | bytes 524288 | tf_op jit(solution)/shard_map/all_to_all | solution.py:190
  1295.4 17.6 %copy-start.16 = (f32[512,512]{1,0:T(8,128)S(1)}, f32[512,512]{1,0:T(8,128)}, u32[]{:S(2)}) copy-start(f32[512,512]{1,0:T(8,128)} %get-tuple-element.217) | copy-start | bytes 3145732
  1315.6 299.6 %copy-start.17 = (f32[512,512]{1,0:T(8,128)}, f32[512,512]{1,0:T(8,128)S(1)}, u32[]{:S(2)}) copy-start(f32[512,512]{1,0:T(8,128)S(1)} %scatter_custom_fusion.3) | copy-start | bytes 3145732
  (101 other events, 306.2 us)
Sparse Core Ops, SparseCore 0:
  11.0 57.9 all-gather.2
  71.9 53.1 all-gather.4
  372.0 311.7 reduce-scatter.10
  724.6 651.1 reduce-scatter.6
  1378.4 132.5 reduce-scatter.8
  1517.8 97.3 reduce-scatter.4
where the time goes:
time: 1650 us; the launch traced here: 1620 us
  starting transfers between devices  528 us (32%)
  waiting for transfers between devices  302 us (18%)
  other arithmetic  266 us (16%)
  local copies, waits for them, and re-layouts  236 us (14%)
  blocking collectives  167 us (10%)
  matrix products  107 us (6%)
    all_to_all x1, starting transfers between devices, local(): lax.all_to_all(returned.astype(jnp.bfloat16), ('band', 'sub'), split_axis...  520 us
    reduce_scatter x1, waiting for transfers between devices, local(): lax.psum_scatter(grad_nw1, ('band', 'sub'), scatter_dimension=0, tiled=True)  135 us
    reduce_scatter x1, waiting for transfers between devices, local(): lax.psum_scatter(grad_ew1, ('band', 'sub'), scatter_dimension=0, tiled=True)  104 us
    unnamed x2, blocking collectives  81.7 us
    reduce_scatter x1, waiting for transfers between devices, local(): lax.psum_scatter(grad_ew2, ('band', 'sub'), scatter_dimension=0, tiled=True)  60.1 us
    scatter-add x8, other arithmetic, backward_step(): jax.ops.segment_sum(djoined[:, 2 * width:], receiver_ids, num_segments=no...  53.7 us
    unnamed x68, local copies, waits for them, and re-layouts  49.4 us
    while x184, local copies, waits for them, and re-layouts  46.8 us
  transfers between devices with their start and end apart: 8, of which 3 were waited for; matrix products, arithmetic and copies ran while one was open for 35% of the time, Pallas kernels for 0%

commit v1 on v0

v1 whole, which is shorter than its diff:
```python
import functools
import jax, jax.numpy as jnp
from jax import lax
from jax.experimental import pallas as pl
from jax.experimental.pallas import tpu as pltpu
from jax.sharding import PartitionSpec as P

EPS = 1e-5
F32 = jnp.float32
BF = jnp.bfloat16

def dot(a, b):
    return jnp.dot(a, b, preferred_element_type=F32)

def dot_t(a, b):
    return lax.dot_general(a, b, (((1,), (1,)), ((), ())), preferred_element_type=F32)

def t_dot(a, b):
    return lax.dot_general(a, b, (((0,), (0,)), ((), ())), preferred_element_type=F32)

def rowmean(v):
    return jnp.sum(v, axis=1, keepdims=True) * (1.0 / v.shape[1])

def norm(v):
    c = v - rowmean(v)
    s = lax.rsqrt(rowmean(c * c) + EPS)
    return c * s, s

def kernel(nb, R, count_ref, sid_ref, rid_ref, e_ref, cot_ref, snd_ref, node_ref, ncot_ref,
           w1_ref, w2_ref, nw1_ref, nw2_ref, vec_ref,
           nout_ref, eout_ref, ngrad_ref, egrad_ref, gw1_ref, gw2_ref, gnw1_ref, gnw2_ref, gvec_ref, sgrad_ref,
           wcat, w2h, hid_s, slope_s, nrm_s, scale_s, gath, dg, gacc, gain_acc, shift_acc):
    i = pl.program_id(0)
    D = e_ref.shape[1]
    S = snd_ref.shape[0]
    N = node_ref.shape[0]
    count = count_ref[0]
    b1 = vec_ref[0:1, :].astype(F32)
    gain = vec_ref[1:2, :].astype(F32)
    shift = vec_ref[2:3, :].astype(F32)

    @pl.when(i == 0)
    def _():
        wcat[0:D, :] = w1_ref[0:D, :] * 0.5
        wcat[D:D + S, :] = (dot(snd_ref[...], w1_ref[D:2 * D, :]) * 0.5).astype(BF)
        wcat[D + S:, :] = ((dot(node_ref[...], w1_ref[2 * D:, :]) + b1) * 0.5).astype(BF)
        w2h[...] = w2_ref[...] * 0.5
        gath[...] = jnp.zeros_like(gath)
        gacc[...] = jnp.zeros_like(gacc)
        gw2_ref[...] = jnp.zeros_like(gw2_ref)
        gain_acc[...] = jnp.zeros_like(gain_acc)
        shift_acc[...] = jnp.zeros_like(shift_acc)

    blk = lax.rem(i, nb)
    first = blk * R
    rows = pl.ds(pl.multiple_of(first, R), R)
    live_blk = first < count

    def onehot_cols(ids_row, width):
        ids = jnp.broadcast_to(ids_row, (128, R)).T
        lane = lax.broadcasted_iota(jnp.int32, (R, 128), 1)
        d = ids - lane
        parts = [jnp.where(d == 128 * j, 1.0, 0.0).astype(BF) for j in range(width // 128)]
        return jnp.concatenate(parts, axis=1)

    def onehot_rows(ids_row, height):
        sub = lax.broadcasted_iota(jnp.int32, (height, R), 0)
        return jnp.where(sub == ids_row, 1.0, 0.0).astype(BF)

    def ids():
        pos = first + lax.broadcasted_iota(jnp.int32, (1, R), 1)
        sid = sid_ref[pl.ds(blk, 1), :]
        rid = jnp.where(pos < count, rid_ref[pl.ds(blk, 1), :], -1)
        return sid, rid

    def live_col():
        return first + lax.broadcasted_iota(jnp.int32, (R, 1), 0) < count

    @pl.when((i < nb) & live_blk)
    def _():
        sid, rid = ids()
        x = jnp.concatenate([e_ref[...], onehot_cols(sid, S), onehot_cols(rid, N)], axis=1)
        h = dot(x, wcat[...])
        a = 1.0 + jnp.tanh(h)
        hid = h * a
        slope = a * (1.0 + 2.0 * h - hid)
        hid = hid.astype(BF)
        hid_s[rows, :] = hid
        slope_s[rows, :] = slope.astype(BF)
        proj = dot(hid, w2_ref[...])
        live = live_col()
        c = proj - rowmean(proj)
        s = lax.rsqrt(rowmean(c * c) + EPS)
        s = jnp.where(live, s, 0.0)
        scale_s[rows, :] = jnp.broadcast_to(s, (R, 128))
        nrm = c * s
        nrm_s[rows, :] = nrm.astype(BF)
        msg = nrm * gain + shift
        eout_ref[...] = (e_ref[...].astype(F32) + jnp.where(live, msg, 0.0)).astype(BF)
        gath[...] += dot(onehot_rows(rid, N), msg.astype(BF))

    @pl.when((i < nb) & jnp.logical_not(live_blk))
    def _():
        eout_ref[...] = e_ref[...]

    @pl.when(i == nb - 1)
    def _():
        nb1 = vec_ref[3:4, :].astype(F32)
        ngain = vec_ref[4:5, :].astype(F32)
        nshift = vec_ref[5:6, :].astype(F32)
        node = node_ref[...]
        g16 = gath[...].astype(BF)
        pre = dot(node, nw1_ref[0:D, :]) + dot(g16, nw1_ref[D:, :]) + nb1
        sig = 0.5 + 0.5 * jnp.tanh(0.5 * pre)
        hid = (pre * sig).astype(BF)
        proj = dot(hid, nw2_ref[...])
        nrm, s = norm(proj)
        nout_ref[...] = (node.astype(F32) + nrm * ngain + nshift).astype(BF)
        up = ncot_ref[...].astype(F32)
        gvec_ref[4:5, :] = jnp.sum(up * nrm, axis=0, keepdims=True)
        gvec_ref[5:6, :] = jnp.sum(up, axis=0, keepdims=True)
        g = up * ngain
        dproj = (s * (g - rowmean(g) - nrm * rowmean(g * nrm))).astype(BF)
        gnw2_ref[...] = t_dot(hid, dproj)
        dpre = dot_t(dproj, nw2_ref[...]) * (sig * (1.0 + pre * (1.0 - sig)))
        dpre16 = dpre.astype(BF)
        gnw1_ref[0:D, :] = t_dot(node, dpre16)
        gnw1_ref[D:, :] = t_dot(g16, dpre16)
        gvec_ref[3:4, :] = jnp.sum(dpre16.astype(F32), axis=0, keepdims=True)
        ngrad_ref[...] = up + dot_t(dpre16, nw1_ref[0:D, :])
        dg[...] = dot_t(dpre16, nw1_ref[D:, :]).astype(BF)

    @pl.when((i >= nb) & live_blk)
    def _():
        sid, rid = ids()
        live = live_col()
        cot = cot_ref[...].astype(F32)
        dm = jnp.where(live, cot, 0.0) + dot(onehot_cols(rid, N), dg[...])
        nrm = nrm_s[rows, :].astype(F32)
        p = dm * nrm
        gain_acc[...] += jnp.sum(p.reshape(R // 8, 8, D), axis=0)
        shift_acc[...] += jnp.sum(dm.reshape(R // 8, 8, D), axis=0)
        g = dm * gain
        m1 = rowmean(g)
        m2 = rowmean(p * gain)
        s = scale_s[rows, 0:1]
        dproj = (s * (g - m1 - nrm * m2)).astype(BF)
        gw2_ref[...] += t_dot(hid_s[rows, :], dproj)
        dpre = (dot_t(dproj, w2h[...]) * slope_s[rows, :].astype(F32)).astype(BF)
        gacc[0:D, :] += t_dot(e_ref[...], dpre)
        gacc[D:D + S, :] += dot(onehot_rows(sid, S), dpre)
        gacc[D + S:, :] += dot(onehot_rows(rid, N), dpre)
        egrad_ref[...] = cot + dot_t(dpre, w1_ref[0:D, :])

    @pl.when((i >= nb) & jnp.logical_not(live_blk))
    def _():
        egrad_ref[...] = cot_ref[...].astype(F32)

    @pl.when(i == 2 * nb - 1)
    def _():
        gvec_ref[1:2, :] = jnp.sum(gain_acc[...], axis=0, keepdims=True)
        gvec_ref[2:3, :] = jnp.sum(shift_acc[...], axis=0, keepdims=True)
        gvec_ref[0:1, :] = jnp.sum(gacc[D + S:, :], axis=0, keepdims=True)
        gvec_ref[6:8, :] = jnp.zeros((2, D), F32)
        us = gacc[D:D + S, :].astype(BF)
        ur = gacc[D + S:, :].astype(BF)
        gw1_ref[0:D, :] = gacc[0:D, :]
        gw1_ref[D:2 * D, :] = t_dot(snd_ref[...], us)
        gw1_ref[2 * D:, :] = t_dot(node_ref[...], ur)
        sgrad_ref[...] = dot_t(us, w1_ref[D:2 * D, :]).astype(BF)
        ngrad_ref[...] += dot_t(ur, w1_ref[2 * D:, :])


def core(count, sid, rid, e, cot, snd, node, ncot, w1, w2, nw1, nw2, vec, R=512):
    E, D = e.shape
    nb = E // R
    S, N = snd.shape[0], node.shape[0]
    V = pl.BlockSpec(memory_space=pltpu.VMEM)
    fb = pl.BlockSpec((R, D), lambda i: (jnp.minimum(i, nb - 1), 0))
    bb = pl.BlockSpec((R, D), lambda i: (jnp.maximum(i - nb, 0), 0))
    both = pl.BlockSpec((R, D), lambda i: (lax.rem(i, nb), 0))
    sds = jax.ShapeDtypeStruct
    return pl.pallas_call(
        functools.partial(kernel, nb, R),
        grid=(2 * nb,),
        in_specs=[pl.BlockSpec(memory_space=pltpu.SMEM), V, V, both, bb, V, V, V, V, V, V, V, V],
        out_specs=[V, fb, V, bb, V, V, V, V, V, V],
        out_shape=[sds((N, D), BF), sds((E, D), BF), sds((N, D), F32), sds((E, D), F32),
                   sds((3 * D, D), F32), sds((D, D), F32), sds((2 * D, D), F32), sds((D, D), F32),
                   sds((8, D), F32), sds((S, D), BF)],
        scratch_shapes=[pltpu.VMEM((D + S + N, D), BF), pltpu.VMEM((D, D), BF),
                        pltpu.VMEM((E, D), BF), pltpu.VMEM((E, D), BF), pltpu.VMEM((E, D), BF),
                        pltpu.VMEM((E, 128), F32), pltpu.VMEM((N, D), F32), pltpu.VMEM((N, D), BF),
                        pltpu.VMEM((D + S + N, D), F32), pltpu.VMEM((8, D), F32), pltpu.VMEM((8, D), F32)],
        compiler_params=pltpu.CompilerParams(vmem_limit_bytes=63 * 1024 * 1024, dimension_semantics=("arbitrary",)),
        name="edge_node_core",
    )(count, sid.reshape(nb, R), rid.reshape(nb, R), e, cot, snd, node, ncot, w1, w2, nw1, nw2, vec)


AXES = ("band", "sub")


def local(node_state, edge_state, send_rows, edge_sender, edge_receiver, edge_count, edge_w1, edge_b1, edge_w2,
          edge_gain, edge_shift, node_w1, node_b1, node_w2, node_gain, node_shift, node_cot, edge_cot):
    D = node_state.shape[1]
    N = node_state.shape[0]
    peers, slots = send_rows.shape[1:]
    mats = (edge_w1, edge_w2, node_w1, node_w2)
    vecs = (edge_b1, edge_gain, edge_shift, node_b1, node_gain, node_shift)
    part = vecs[0].shape[0]
    w1, w2, nw1, nw2 = (lax.all_gather(m, AXES, axis=0, tiled=True) for m in mats)
    vec = lax.all_gather(jnp.stack(vecs), AXES, axis=1, tiled=True)
    vec = jnp.concatenate([vec, jnp.zeros((2, D), BF)], axis=0)
    selected = send_rows[0].reshape(peers * slots)
    outgoing = jnp.take(node_state, selected, axis=0).reshape(peers, slots, D)
    senders = lax.all_to_all(outgoing, AXES, split_axis=0, concat_axis=0, tiled=True).reshape(peers * slots, D)
    node_out, edge_out, node_grad, edge_grad, gw1, gw2, gnw1, gnw2, gvec, sgrad = core(
        edge_count, edge_sender, edge_receiver, edge_state, edge_cot, senders, node_state, node_cot,
        w1, w2, nw1, nw2, vec)
    arrived = lax.all_to_all(sgrad.reshape(peers, slots, D), AXES, split_axis=0, concat_axis=0, tiled=True)
    node_grad = node_grad + jax.ops.segment_sum(
        arrived.reshape(peers * slots, D).astype(F32), selected, num_segments=N)

    def scatter(v):
        return lax.psum_scatter(v, AXES, scatter_dimension=0, tiled=True)

    gw1, gw2, gnw1, gnw2 = (scatter(v) for v in (gw1, gw2, gnw1, gnw2))
    gv = lax.psum_scatter(gvec, AXES, scatter_dimension=1, tiled=True)
    return (node_out, edge_out, node_grad, edge_grad, gw1, gv[0], gw2, gv[1], gv[2], gnw1, gv[3], gnw2, gv[4], gv[5])


def solution(mesh):
    two, one, three = P(AXES, None), P(AXES), P(AXES, None, None)
    in_specs = (two, two, three, one, one, one, two, one, two, one, one, two, one, two, one, one, two, two)
    out_specs = (two, two, two, two, two, one, two, one, one, two, one, two, one, one)
    return jax.shard_map(local, mesh=mesh, in_specs=in_specs, out_specs=out_specs, check_vma=False)
```

time: 1650 us -> 890 us (0.54); the launches traced: 1620 us -> 889 us
  starting transfers between devices: 528 us -> 10.2 us
  waiting for transfers between devices: 302 us -> 631 us
  other arithmetic: 266 us -> 4.05 us
  local copies, waits for them, and re-layouts: 236 us -> 14.4 us
  matrix products: 107 us -> 0 us
  Pallas kernels: 0 us -> 88.6 us
  blocking collectives: 167 us -> 126 us
    all_to_all x2, starting transfers between devices: 528 us -> 9.9 us  [the longest x1 7.3 us: local(): lax.all_to_all(outgoing, AXES, split_axis=0, concat_axis=0, tiled=True)]
    reduce_scatter x4, waiting for transfers between devices: 300 us -> 502 us  [scatter(): return lax.psum_scatter(v, AXES, scatter_dimension=0, tiled=True)]
    unnamed x6 -> x8, waiting for transfers between devices: 1.95 us -> 129 us
    scatter-add x25 -> x1, other arithmetic: 125 us -> 2.54 us  [local(): jax.ops.segment_sum(arrived.reshape(peers * slots, D).astype(F32), select...]
    dot_general x62 -> x0, matrix products: 107 us -> none  [the longest x16 32.1 us: edge_front(): projected = jnp.dot(hidden, full_ew2, preferred_element_type=flt)]
    gather x65 -> x1, local copies, waits for them, and re-layouts: 92 us -> 2.32 us  [local(): outgoing = jnp.take(node_state, selected, axis=0).reshape(peers, slots, D)]
    pallas_call x0 -> x1, Pallas kernels: none -> 88.6 us  [core(): pl.pallas_call(functools.partial(kernel, nb, R), grid=(2 * nb,), in_specs...]
    unnamed x2 -> x0, blocking collectives: 81.7 us -> none
  transfers between devices with their start and end apart: 8 -> 9, of which waited for: 3 -> 5; matrix products, arithmetic and copies ran while one was open for 35% -> 2% of each run, Pallas kernels for 0% -> 0%
where the time goes in v1:
time: 890 us; the launch traced here: 889 us
  waiting for transfers between devices  631 us (71%)
  blocking collectives  126 us (14%)
  Pallas kernels  88.6 us (10%)
  between operations  14.9 us (2%)
  local copies, waits for them, and re-layouts  14.4 us (2%)
  starting transfers between devices  10.2 us (1%)
    reduce_scatter x4, waiting for transfers between devices, scatter(): return lax.psum_scatter(v, AXES, scatter_dimension=0, tiled=True)  502 us
    unnamed x8, waiting for transfers between devices  129 us
    pallas_call x1, Pallas kernels, core(): pl.pallas_call(functools.partial(kernel, nb, R), grid=(2 * nb,), in_specs...  88.6 us
    all_gather x2, blocking collectives, local(): lax.all_gather(m, AXES, axis=0, tiled=True)  83.7 us
    all_gather x1, blocking collectives, local(): vec = lax.all_gather(jnp.stack(vecs), AXES, axis=1, tiled=True)  42 us
  transfers between devices with their start and end apart: 9, of which 5 were waited for; matrix products, arithmetic and copies ran while one was open for 2% of the time, Pallas kernels for 0%

profile of v1, /device:TPU:0, one launch (start us, length us, event | category | flops | bytes accessed | tf_op | source)
XLA Modules:
  0.0 889.0 jit_solution(4595092774320044777)
XLA Ops:
  7.2 0.7 all-gather.6.cloned.1.call-update
  8.0 0.7 all-gather.4.cloned.1.call-update
  8.7 0.8 copy.39
  9.4 0.7 compare_and_fusion
  10.3 2.3 gather_fusion
  12.7 0.8 bitcast_select_fusion
  13.5 7.3 all-to-all-start
  21.5 1.4 reshape.84.sid_ref
  22.8 1.4 reshape.85.rid_ref
  24.2 0.8 stack.27
  25.0 42.0 %all-gather = bf16[32,16,6]{1,2,0:T(8,128)(2,1)S(1)} all-gather(bf16[1,16,6]{1,2,0:T(8,128)(2,1)S(1)} %bitcast.40), channel_id=1, replica_groups=mesh['band'=16,'sub'=2] {'band','sub'}, dimensions={0}, use_global_device_ids=true | all-gather | bytes 6336 | tf_op jit(solution)/shard_map/all_gather | solution.py:212
  67.7 41.4 %all_gather.16.w2_ref = bf16[512,512]{1,0:T(8,128)(2,1)} all-gather(bf16[16,512]{1,0:T(8,128)(2,1)} %param.26), channel_id=1, replica_groups=mesh['band'=16,'sub'=2] {'band','sub'}, dimensions={0}, use_global_device_ids=true | all-gather | bytes 540672 | tf_op jit(solution)/shard_map/all_gather | solution.py:211
  109.1 42.3 %all_gather.18.nw2_ref = bf16[512,512]{1,0:T(8,128)(2,1)} all-gather(bf16[16,512]{1,0:T(8,128)(2,1)} %param.31), channel_id=1, replica_groups=mesh['band'=16,'sub'=2] {'band','sub'}, dimensions={0}, use_global_device_ids=true | all-gather | bytes 540672 | tf_op jit(solution)/shard_map/all_gather | solution.py:211
  152.2 88.6 %edge_node_core.1 = (bf16[512,512]{1,0:T(8,128)(2,1)}, bf16[8192,512]{1,0:T(8,128)(2,1)}, f32[512,512]{1,0:T(8,128)}, f32[8192,512]{1,0:T(8,128)}, f32[1536,512]...) custom-call(s32[1]{0:T(128)S(6)} %copy.51.count_ref, ...), custom_call_target="tpu_custom_call" | custom-call | tf_op jit(solution)/shard_map/edge_node_core/pallas_call | solution.py:183
  240.8 1.7 copy.42
  244.3 0.7 reduce-scatter.12.cloned.1.call-update
  245.0 2.6 all-to-all-start.1
  247.7 125.1 %reduce-scatter.16.cloned.1.call-done = f32[16,8]{1,0:T(8,128)} async-done(((f32[512,8]{1,0:T(8,128)}), f32[16,8]{1,0:T(8,128)}) %reduce-scatter.16.cloned.1.call-update) | async-done | bytes 528
  372.8 1.0 fusion.3
  377.3 2.5 scatter_custom_fusion
  379.8 126.4 %reduce-scatter.10.cloned.1.call-done = f32[16,512]{1,0:T(8,128)} async-done(((f32[512,512]{1,0:T(8,128)}), f32[16,512]{1,0:T(8,128)}) %reduce-scatter.10.cloned.1.call-update) | async-done | bytes 32784 | tf_op jit(solution)/shard_map/reduce_scatter | solution.py:225
  506.3 133.4 %reduce-scatter.14.cloned.1.call-done = f32[16,512]{1,0:T(8,128)} async-done(((f32[512,512]{1,0:T(8,128)}), f32[16,512]{1,0:T(8,128)}) %reduce-scatter.14.cloned.1.call-update) | async-done | bytes 32784 | tf_op jit(solution)/shard_map/reduce_scatter | solution.py:225
  639.7 104.2 %reduce-scatter.8.cloned.1.call-done = f32[48,512]{1,0:T(8,128)} async-done(((f32[1536,512]{1,0:T(8,128)}), f32[48,512]{1,0:T(8,128)}) %reduce-scatter.8.cloned.1.call-update) | async-done | bytes 98320 | tf_op jit(solution)/shard_map/reduce_scatter | solution.py:225
  744.0 138.2 %reduce-scatter.12.cloned.1.call-done = f32[32,512]{1,0:T(8,128)} async-done(((f32[1024,512]{1,0:T(8,128)}), f32[32,512]{1,0:T(8,128)}) %reduce-scatter.12.cloned.1.call-update) | async-done | bytes 65552 | tf_op jit(solution)/shard_map/reduce_scatter | solution.py:225
  (35 shorter events, 7.1 us)
Async XLA Ops:
  7.2 144.3 %all-gather.6.cloned.1.call-start = ((), (), s32[]{:S(2)}) async-start(), calls=%async_computation.8 | async-start | bytes 1081344 | tf_op jit(solution)/shard_map/all_gather | solution.py:211
  7.9 143.6 %all-gather.4.cloned.1.call-start = ((), (), s32[]{:S(2)}) async-start(), calls=%async_computation.7 | async-start | bytes 1622016 | tf_op jit(solution)/shard_map/all_gather | solution.py:211
  13.5 138.0 %all-to-all-start = ((bf16[32,8,512]{2,1,0:T(8,128)(2,1)}), bf16[32,8,512]{2,1,0:T(8,128)(2,1)S(1)}, u32[]{:S(2)}, u32[]{:S(2)}) async-start(bf16[32,8,512]{2,1,0:T(8,128)(2,1)} %bitcast_select_fusion), calls=%async_computation | async-start | bytes 524288 | tf_op jit(solution)/shard_map/all_to_all | solution.py:216
  20.8 352.0 %reduce-scatter.16.cloned.1.call-start = ((), (), s32[]{:S(2)}) async-start(), calls=%async_computation.13 | async-start | bytes 270336
  151.5 0.7 copy-start
  240.8 136.5 %copy-start.1 = (f32[512,512]{1,0:T(8,128)S(1)}, f32[512,512]{1,0:T(8,128)}, u32[]{:S(2)}) copy-start(f32[512,512]{1,0:T(8,128)} %get-tuple-element.26) | copy-start | bytes 3145732
  242.5 263.8 %reduce-scatter.10.cloned.1.call-start = ((), (), s32[]{:S(2)}) async-start(), calls=%async_computation.10 | async-start | bytes 1081344 | tf_op jit(solution)/shard_map/reduce_scatter | solution.py:225
  243.1 396.6 %reduce-scatter.14.cloned.1.call-start = ((), (), s32[]{:S(2)}) async-start(), calls=%async_computation.12 | async-start | bytes 1081344 | tf_op jit(solution)/shard_map/reduce_scatter | solution.py:225
  243.7 500.3 %reduce-scatter.8.cloned.1.call-start = ((), (), s32[]{:S(2)}) async-start(), calls=%async_computation.9 | async-start | bytes 3244032 | tf_op jit(solution)/shard_map/reduce_scatter | solution.py:225
  244.2 637.9 %reduce-scatter.12.cloned.1.call-start = ((), (), s32[]{:S(2)}) async-start(), calls=%async_computation.11 | async-start | bytes 2162688 | tf_op jit(solution)/shard_map/reduce_scatter | solution.py:225
  245.0 132.3 %all-to-all-start.1 = ((bf16[32,8,512]{2,1,0:T(8,128)(2,1)}), bf16[32,8,512]{2,1,0:T(8,128)(2,1)S(1)}, u32[]{:S(2)}, u32[]{:S(2)}) async-start(bf16[32,8,512]{2,1,0:T(8,128)(2,1)} %bitcast.38), calls=%async_computation.1 | async-start | bytes 524288 | tf_op jit(solution)/shard_map/all_to_all | solution.py:220
  379.8 502.3 %copy-start.2 = (f32[512,512]{1,0:T(8,128)}, f32[512,512]{1,0:T(8,128)S(1)}, u32[]{:S(2)}) copy-start(f32[512,512]{1,0:T(8,128)S(1)} %scatter_custom_fusion) | copy-start | bytes 3145732
Sparse Core Ops, SparseCore 0:
  10.9 56.7 all-gather.5
  70.6 54.7 all-gather.3
  242.6 130.1 reduce-scatter.15
  375.5 130.6 reduce-scatter.9
  508.9 130.7 reduce-scatter.13
  646.5 97.4 reduce-scatter.7
  746.9 135.1 reduce-scatter.11

commit v2 on v1

--- a/solution.py
+++ b/solution.py
@@ -5,9 +5,411 @@
 from jax.experimental.pallas import tpu as pltpu
 from jax.sharding import PartitionSpec as P
 
-EPS = 1e-5
 F32 = jnp.float32
 BF = jnp.bfloat16
+AXES = ("band", "sub")
+MESH = pl.DeviceIdType.MESH
+LINE = 4
+
+
+def up16(n):
+    return -(-n // 16) * 16
+
+
+def layout(parts):
+    spots, at = [], 0
+    for p in parts:
+        spots.append(at)
+        at += 4 * up16(p)
+    return spots, at
+
+
+class Place:
+    def __init__(self, bands):
+        self.bands = bands
+        self.quads = bands // LINE
+        band, self.c = lax.axis_index("band"), lax.axis_index("sub")
+        self.a, self.q = band // LINE, band % LINE
+        x, y = self.q % 2, self.q // 2
+        self.qx = self.q + 1 - 2 * x
+        self.qy = self.q + 2 - 4 * y
+        self.qd = 3 - self.q
+        self.me = band * 2 + self.c
+        self.devices = bands * 2
+
+    def dev(self, a, q, c):
+        return (a * LINE + q, c)
+
+    def idx(self, a, q, c):
+        return (a * LINE + q) * 2 + c
+
+    def other_a(self, k):
+        return (self.a + k) % self.quads
+
+
+def barrier_all(pos):
+    sem = pltpu.get_barrier_semaphore()
+
+    @pl.loop(1, pos.devices)
+    def _(k):
+        t = (pos.me + k) % pos.devices
+        pl.semaphore_signal(sem, inc=1, device_id=(t // 2, t % 2), device_id_type=MESH)
+
+    pl.semaphore_wait(sem, pos.devices - 1)
+
+
+def gather_kernel(bands, parts, fast, w1_ref, w2_ref, nw1_ref, nw2_ref, vec_ref, sel_ref, node_ref, *refs):
+    if fast:
+        outs, (vec_out, snd_out, buf, outg, inc, recv, half, send, a_recv, a_send) = refs[:4], refs[4:]
+    else:
+        (buf, vec_out, snd_out, outg, inc, recv, half, send, a_recv, a_send) = refs
+        outs = None
+    pos = Place(bands)
+    spots, tail = layout(parts)
+    rows = buf.shape[1]
+    cut = up16(rows // 2)
+    me, c, a, q = pos.me, pos.c, pos.a, pos.q
+    mats = (w1_ref, w2_ref, nw1_ref, nw2_ref)
+    D = node_ref.shape[1]
+    peers, slots = sel_ref.shape
+    S = peers * slots
+    for m, p, o in zip(mats, parts, spots):
+        for j in range(4):
+            buf[me, o + j * up16(p):o + j * up16(p) + p, :] = m[:, 128 * j:128 * j + 128]
+    group = 128 // vec_ref.shape[1]
+    lanes = lax.broadcasted_iota(jnp.int32, (8, 128), 1)
+    vals = jnp.concatenate([vec_ref[...]] * group, axis=1).astype(F32)
+    vals = jnp.where(lanes // vec_ref.shape[1] == me % group, vals, 0.0)
+    buf[me, tail:tail + 16, :] = jnp.concatenate([vals, jnp.zeros((8, 128), F32)], axis=0).astype(BF)
+    barrier_all(pos)
+    count = [0]
+
+    def push(src, part, sem, target):
+        ref = buf.at[src] if part is None else buf.at[src, part]
+        cp = pltpu.make_async_remote_copy(src_ref=ref, dst_ref=ref, send_sem=send.at[count[0]], recv_sem=sem,
+                                          device_id=target, device_id_type=MESH)
+        count[0] += 1
+        cp.start()
+        return cp
+
+    started = []
+    A_PART, B_PART = pl.ds(0, cut), pl.ds(cut, rows - cut)
+
+    def wait(src, part, sem):
+        ref = buf.at[src] if part is None else buf.at[src, part]
+        pltpu.make_async_remote_copy(src_ref=ref, dst_ref=ref, send_sem=send.at[0], recv_sem=sem,
+                                     device_id=pos.dev(a, q, 1 - c), device_id_type=MESH).wait_recv()
+
+    def unpack(src):
+        if outs is None:
+            return
+        for o_ref, p, o in zip(outs, parts, spots):
+            for j in range(4):
+                o_ref[pl.ds(pl.multiple_of(src * p, 16), p), 128 * j:128 * j + 128] = \
+                    buf[src, o + j * p:o + j * p + p, :]
+
+    for k in range(1, pos.quads):
+        started.append(push(me, None, recv.at[me], pos.dev(pos.other_a(k), q, c)))
+
+    def spread(src):
+        started.append(push(src, None, recv.at[src], pos.dev(a, pos.qx, c)))
+        started.append(push(src, None, recv.at[src], pos.dev(a, pos.qy, c)))
+
+    def sibling(src):
+        started.append(push(src, None, recv.at[src], pos.dev(a, q, 1 - c)))
+
+    spread(me)
+    sibling(me)
+    ids = sel_ref[...]
+    pick = (lax.broadcasted_iota(jnp.int32, (S, peers), 0) // slots
+            == lax.broadcasted_iota(jnp.int32, (S, peers), 1)).astype(BF)
+    low = jnp.dot(pick, (ids % 256).astype(BF), preferred_element_type=F32)
+    high = jnp.dot(pick, (ids // 256).astype(BF), preferred_element_type=F32)
+    mine = lax.broadcasted_iota(jnp.int32, (S, slots), 0) % slots == lax.broadcasted_iota(jnp.int32, (S, slots), 1)
+    col = jnp.sum(jnp.where(mine, low + 256.0 * high, 0.0), axis=1, keepdims=True)
+    hot = (col == lax.broadcasted_iota(jnp.int32, (S, node_ref.shape[0]), 1).astype(F32)).astype(BF)
+    picked = jnp.dot(hot, node_ref[...], preferred_element_type=F32)
+    outg[:, 0:slots, :] = picked[:, 0:D // 2].reshape(peers, slots, D // 2).astype(BF)
+    outg[:, slots:, :] = picked[:, D // 2:].reshape(peers, slots, D // 2).astype(BF)
+
+    def exchange(t):
+        return pltpu.make_async_remote_copy(src_ref=outg.at[t], dst_ref=inc.at[me], send_sem=a_send.at[t],
+                                            recv_sem=a_recv.at[me], device_id=(t // 2, t % 2), device_id_type=MESH)
+
+    @pl.loop(1, pos.devices)
+    def _(k):
+        exchange((me + k) % pos.devices).start()
+
+    inc[me] = outg[me]
+    unpack(me)
+    line = [pos.idx(pos.other_a(k), q, c) for k in range(1, pos.quads)]
+    for src in line:
+        wait(src, None, recv.at[src])
+        spread(src)
+        sibling(src)
+        unpack(src)
+    for k in range(pos.quads):
+        ak = pos.other_a(k)
+        sx, sy = pos.idx(ak, pos.qx, c), pos.idx(ak, pos.qy, c)
+        wait(sx, None, recv.at[sx])
+        started.append(push(sx, A_PART, half.at[0, ak], pos.dev(a, pos.qy, c)))
+        sibling(sx)
+        unpack(sx)
+        wait(sy, None, recv.at[sy])
+        started.append(push(sy, B_PART, half.at[1, ak], pos.dev(a, pos.qx, c)))
+        sibling(sy)
+        unpack(sy)
+    for k in range(pos.quads):
+        ak = pos.other_a(k)
+        sd = pos.idx(ak, pos.qd, c)
+        wait(sd, A_PART, half.at[0, ak])
+        wait(sd, B_PART, half.at[1, ak])
+        sibling(sd)
+        unpack(sd)
+
+    @pl.loop(1, pos.devices)
+    def _(k):
+        t = (me + k) % pos.devices
+        pltpu.make_async_remote_copy(src_ref=outg.at[t], dst_ref=inc.at[t], send_sem=a_send.at[t],
+                                     recv_sem=a_recv.at[t], device_id=(t // 2, t % 2), device_id_type=MESH).wait()
+
+    snd_out[:, 0:D // 2] = inc[:, 0:slots, :].astype(F32).reshape(S, D // 2).astype(BF)
+    snd_out[:, D // 2:] = inc[:, slots:, :].astype(F32).reshape(S, D // 2).astype(BF)
+    for k in range(pos.quads):
+        ak = pos.other_a(k)
+        for qq in (q, pos.qx, pos.qy, pos.qd):
+            src = pos.idx(ak, qq, 1 - c)
+            wait(src, None, recv.at[src])
+            unpack(src)
+    for g in range(D // 128):
+        v = buf[g * group, tail:tail + 16, :].astype(F32)
+        for s in range(1, group):
+            v = v + buf[g * group + s, tail:tail + 16, :].astype(F32)
+        vec_out[:, 128 * g:128 * g + 128] = v.astype(BF)
+    for cp in started:
+        cp.wait_send()
+
+
+def gather_weights(bands, w1, w2, nw1, nw2, vec, sel, node):
+    parts = tuple(m.shape[0] for m in (w1, w2, nw1, nw2))
+    fast = all(p % 16 == 0 for p in parts)
+    _, tail = layout(parts)
+    rows = tail + 16
+    n = bands * 2
+    quads = bands // LINE
+    D = node.shape[1]
+    peers, slots = sel.shape
+    S = peers * slots
+    V = pl.BlockSpec(memory_space=pltpu.VMEM)
+    sds = jax.ShapeDtypeStruct
+    shards = sds((n, rows, 128), BF)
+    full = [sds((n * p, D), BF) for p in parts]
+    outs = (full if fast else [shards]) + [sds((16, D), BF), sds((S, D), BF)]
+    sends = (quads - 1) + 2 * quads + 2 * quads + 4 * quads
+    scratch = ([pltpu.VMEM(shards.shape, BF)] if fast else []) + [
+        pltpu.VMEM((peers, 2 * slots, D // 2), BF), pltpu.VMEM((peers, 2 * slots, D // 2), BF),
+        pltpu.SemaphoreType.DMA((n,)), pltpu.SemaphoreType.DMA((2, quads)), pltpu.SemaphoreType.DMA((sends,)),
+        pltpu.SemaphoreType.DMA((n,)), pltpu.SemaphoreType.DMA((n,))]
+    res = pl.pallas_call(
+        functools.partial(gather_kernel, bands, parts, fast),
+        out_shape=outs, in_specs=[V] * 7, out_specs=[V] * len(outs), scratch_shapes=scratch,
+        compiler_params=pltpu.CompilerParams(collective_id=0, has_side_effects=True, vmem_limit_bytes=60 * 2**20),
+        name="gather_weights",
+    )(w1, w2, nw1, nw2, vec, sel, node)
+    if fast:
+        return res
+    got, vec, snd = res
+    spots, _ = layout(parts)
+    mats = []
+    for p, o in zip(parts, spots):
+        cols = [got[:, o + j * up16(p):o + j * up16(p) + p, :].reshape(n * p, 128) for j in range(4)]
+        mats.append(jnp.concatenate(cols, axis=1))
+    return (*mats, vec, snd)
+
+
+def reduce_kernel(bands, p_ref, msg_ref, red_ref, arr_ref, own, sib, xa, yb, ya, xb, zin,
+                  own_sem, sib_recv, x1, y1, y2, x2, z_recv, send, a_recv, a_send):
+    pos = Place(bands)
+    me, c, a, q = pos.me, pos.c, pos.a, pos.q
+    rows = own.shape[1]
+    cut = up16(rows // 2)
+    A, B = pl.ds(0, cut), pl.ds(cut, rows - cut)
+    count = [0]
+    started = []
+
+    def push(src, dst, sem, target):
+        cp = pltpu.make_async_remote_copy(src_ref=src, dst_ref=dst, send_sem=send.at[count[0]], recv_sem=sem,
+                                          device_id=target, device_id_type=MESH)
+        count[0] += 1
+        cp.start()
+        started.append(cp)
+
+    def wait(dst, sem):
+        pltpu.make_async_remote_copy(src_ref=dst, dst_ref=dst, send_sem=send.at[0], recv_sem=sem,
+                                     device_id=pos.dev(a, q, 1 - c), device_id_type=MESH).wait_recv()
+
+    order = [pos.other_a(k) for k in range(1, pos.quads)] + [a]
+    square = [pl.ds(ak * LINE, LINE) for ak in order]
+    mine = []
+    for ak, sq in zip(order, square):
+        cp = pltpu.make_async_copy(p_ref.at[c, sq], own.at[sq], own_sem.at[ak])
+        cp.start()
+        mine.append(cp)
+    barrier_all(pos)
+    for ak, sq in zip(order, square):
+        push(p_ref.at[1 - c, sq], sib.at[sq], sib_recv.at[ak], pos.dev(a, q, 1 - c))
+
+    def exchange(t):
+        return pltpu.make_async_remote_copy(src_ref=msg_ref.at[t], dst_ref=arr_ref.at[me], send_sem=a_send.at[t],
+                                            recv_sem=a_recv.at[me], device_id=(t // 2, t % 2), device_id_type=MESH)
+
+    @pl.loop(1, pos.devices)
+    def _(k):
+        exchange((me + k) % pos.devices).start()
+
+    arr_ref[me] = msg_ref[me]
+    to_x, to_y = pos.dev(a, pos.qx, c), pos.dev(a, pos.qy, c)
+
+    def add(ref, idx, other):
+        ref[idx] = (ref[idx].astype(F32) + other.astype(F32)).astype(BF)
+
+    def first(k):
+        ak, sq = order[k], square[k]
+        at = ak * LINE
+        mine[k].wait()
+        wait(sib.at[sq], sib_recv.at[ak])
+        own[sq] = (own[sq].astype(F32) + sib[sq].astype(F32)).astype(BF)
+        push(own.at[at + pos.qx, A], xa.at[ak, 0], x1.at[ak, 0], to_x)
+        push(own.at[at + pos.qy, B], yb.at[ak, 0], y1.at[ak, 0], to_y)
+        push(own.at[at + pos.qd, A], xa.at[ak, 1], x1.at[ak, 1], to_x)
+        push(own.at[at + pos.qd, B], yb.at[ak, 1], y1.at[ak, 1], to_y)
+
+    def second(k):
+        ak = order[k]
+        at = ak * LINE
+        wait(xa.at[ak, 1], x1.at[ak, 1])
+        add(own, (at + pos.qy, A), xa[ak, 1])
+        push(own.at[at + pos.qy, A], ya.at[ak], y2.at[ak], to_y)
+        wait(yb.at[ak, 1], y1.at[ak, 1])
+        add(own, (at + pos.qx, B), yb[ak, 1])
+        push(own.at[at + pos.qx, B], xb.at[ak], x2.at[ak], to_x)
+
+    def third(k):
+        ak = order[k]
+        at = ak * LINE
+        wait(xa.at[ak, 0], x1.at[ak, 0])
+        wait(yb.at[ak, 0], y1.at[ak, 0])
+        wait(ya.at[ak], y2.at[ak])
+        wait(xb.at[ak], x2.at[ak])
+        top = own[at + q, A].astype(F32) + xa[ak, 0].astype(F32) + ya[ak].astype(F32)
+        low = own[at + q, B].astype(F32) + yb[ak, 0].astype(F32) + xb[ak].astype(F32)
+        if k < pos.quads - 1:
+            own[at + q, A] = top.astype(BF)
+            own[at + q, B] = low.astype(BF)
+            push(own.at[at + q], zin.at[a], z_recv.at[a], pos.dev(ak, q, c))
+        else:
+            red_ref[A, :] = top
+            red_ref[B, :] = low
+
+    n = pos.quads
+    first(0)
+    if n > 1:
+        first(1)
+    for k in range(n):
+        second(k)
+        if k + 2 < n:
+            first(k + 2)
+        if k >= 1:
+            third(k - 1)
+    third(n - 1)
+    for k in range(n - 1):
+        ak = order[k]
+        wait(zin.at[ak], z_recv.at[ak])
+        red_ref[...] += zin[ak].astype(F32)
+
+    @pl.loop(1, pos.devices)
+    def _(k):
+        t = (me + k) % pos.devices
+        pltpu.make_async_remote_copy(src_ref=msg_ref.at[t], dst_ref=arr_ref.at[t], send_sem=a_send.at[t],
+                                     recv_sem=a_recv.at[t], device_id=(t // 2, t % 2), device_id_type=MESH).wait()
+
+    for cp in started:
+        cp.wait_send()
+
+
+def reduce_grads(bands, packed, msgs):
+    rows = packed.shape[2]
+    n = bands * 2
+    quads = bands // LINE
+    cut = up16(rows // 2)
+    V = pl.BlockSpec(memory_space=pltpu.VMEM)
+    sds = jax.ShapeDtypeStruct
+    sem = pltpu.SemaphoreType.DMA
+    return pl.pallas_call(
+        functools.partial(reduce_kernel, bands),
+        out_shape=[sds((rows, 128), F32), sds(msgs.shape, BF)],
+        in_specs=[pl.BlockSpec(memory_space=pl.ANY), V], out_specs=[V, V],
+        scratch_shapes=[
+            pltpu.VMEM((bands, rows, 128), BF), pltpu.VMEM((bands, rows, 128), BF),
+            pltpu.VMEM((quads, 2, cut, 128), BF), pltpu.VMEM((quads, 2, rows - cut, 128), BF),
+            pltpu.VMEM((quads, cut, 128), BF), pltpu.VMEM((quads, rows - cut, 128), BF),
+            pltpu.VMEM((quads, rows, 128), BF),
+            sem((quads,)), sem((quads,)), sem((quads, 2)), sem((quads, 2)), sem((quads,)), sem((quads,)), sem((quads,)),
+            sem((8 * quads,)), sem((n,)), sem((n,))],
+        compiler_params=pltpu.CompilerParams(collective_id=1, has_side_effects=True, vmem_limit_bytes=60 * 2**20),
+        name="reduce_grads",
+    )(packed, msgs)
+
+
+def finish_kernel(bands, parts, red_ref, arr_ref, sel_ref, part_ref, ngrad_ref, w1_ref, w2_ref, nw1_ref, nw2_ref, *vecs):
+    me = lax.axis_index("band") * 2 + lax.axis_index("sub")
+    spots, tail = layout(parts)
+    for o_ref, p, o in zip((w1_ref, w2_ref, nw1_ref, nw2_ref), parts, spots):
+        for j in range(4):
+            o_ref[:, 128 * j:128 * j + 128] = red_ref[o + j * up16(p):o + j * up16(p) + p, :]
+    width = vecs[0].shape[0]
+    group = 128 // width
+    slab = red_ref[tail:tail + 8, :]
+    got = slab[:, 0:width]
+    for g in range(1, group):
+        got = jnp.where(me % group == g, slab[:, g * width:(g + 1) * width], got)
+    for k, v_ref in enumerate(vecs):
+        v_ref[...] = got[k]
+    peers, slots = sel_ref.shape
+    S = peers * slots
+    N, D = part_ref.shape
+    hot = slot_onehot(sel_ref[...], N)
+    arrived = jnp.concatenate([arr_ref[:, 0:slots, :].astype(F32).reshape(S, D // 2),
+                               arr_ref[:, slots:, :].astype(F32).reshape(S, D // 2)], axis=1).astype(BF)
+    ngrad_ref[...] = part_ref[...] + lax.dot_general(hot, arrived, (((0,), (0,)), ((), ())), preferred_element_type=F32)
+
+
+def slot_onehot(ids, nodes):
+    peers, slots = ids.shape
+    S = peers * slots
+    pick = (lax.broadcasted_iota(jnp.int32, (S, peers), 0) // slots
+            == lax.broadcasted_iota(jnp.int32, (S, peers), 1)).astype(BF)
+    low = jnp.dot(pick, (ids % 256).astype(BF), preferred_element_type=F32)
+    high = jnp.dot(pick, (ids // 256).astype(BF), preferred_element_type=F32)
+    mine = lax.broadcasted_iota(jnp.int32, (S, slots), 0) % slots == lax.broadcasted_iota(jnp.int32, (S, slots), 1)
+    col = jnp.sum(jnp.where(mine, low + 256.0 * high, 0.0), axis=1, keepdims=True)
+    return (col == lax.broadcasted_iota(jnp.int32, (S, nodes), 1).astype(F32)).astype(BF)
+
+
+def finish(bands, parts, width, red, arrived, sel, part):
+    V = pl.BlockSpec(memory_space=pltpu.VMEM)
+    sds = jax.ShapeDtypeStruct
+    D = part.shape[1]
+    outs = [sds(part.shape, F32)] + [sds((p, D), F32) for p in parts] + [sds((width,), F32)] * 6
+    return pl.pallas_call(
+        functools.partial(finish_kernel, bands, parts),
+        out_shape=outs, in_specs=[V] * 4, out_specs=[V] * len(outs),
+        compiler_params=pltpu.CompilerParams(vmem_limit_bytes=60 * 2**20),
+        name="finish",
+    )(red, arrived, sel, part)
+
+
+EPS = 1e-5
 
 def dot(a, b):
     return jnp.dot(a, b, preferred_element_type=F32)
@@ -26,10 +428,12 @@
     s = lax.rsqrt(rowmean(c * c) + EPS)
     return c * s, s
 
-def kernel(nb, R, count_ref, sid_ref, rid_ref, e_ref, cot_ref, snd_ref, node_ref, ncot_ref,
+def core_kernel(nb, R, parts, count_ref, sid_ref, rid_ref, e_ref, cot_ref, snd_ref, node_ref, ncot_ref,
            w1_ref, w2_ref, nw1_ref, nw2_ref, vec_ref,
-           nout_ref, eout_ref, ngrad_ref, egrad_ref, gw1_ref, gw2_ref, gnw1_ref, gnw2_ref, gvec_ref, sgrad_ref,
-           wcat, w2h, hid_s, slope_s, nrm_s, scale_s, gath, dg, gacc, gain_acc, shift_acc):
+           nout_ref, eout_ref, ngrad_ref, egrad_ref, msg_ref, *refs):
+    fast = all(p % 16 == 0 for p in parts)
+    pack_ref = refs[0] if fast else None
+    (gw1_ref, gw2_ref, gnw1_ref, gnw2_ref, gvec_ref, wcat, w2h, hid_s, slope_s, nrm_s, scale_s, gath, dg, gacc, gain_acc, shift_acc) = refs[fast:]
     i = pl.program_id(0)
     D = e_ref.shape[1]
     S = snd_ref.shape[0]
@@ -167,11 +571,34 @@
         gw1_ref[0:D, :] = gacc[0:D, :]
         gw1_ref[D:2 * D, :] = t_dot(snd_ref[...], us)
         gw1_ref[2 * D:, :] = t_dot(node_ref[...], ur)
-        sgrad_ref[...] = dot_t(us, w1_ref[D:2 * D, :]).astype(BF)
+        sgrad = dot_t(us, w1_ref[D:2 * D, :])
+        peers, slots = msg_ref.shape[0], msg_ref.shape[1] // 2
+        msg_ref[:, 0:slots, :] = sgrad[:, 0:D // 2].reshape(peers, slots, D // 2).astype(BF)
+        msg_ref[:, slots:, :] = sgrad[:, D // 2:].reshape(peers, slots, D // 2).astype(BF)
         ngrad_ref[...] += dot_t(ur, w1_ref[2 * D:, :])
-
-
-def core(count, sid, rid, e, cot, snd, node, ncot, w1, w2, nw1, nw2, vec, R=512):
+        if not fast:
+            return
+        spots, tail = layout(parts)
+        bands = pack_ref.shape[1]
+        group = 2 * bands // (D // 128)
+
+        @pl.loop(0, bands)
+        def _(b):
+            for c in range(2):
+                d = b * 2 + c
+                for g_ref, p, o in zip((gw1_ref, gw2_ref, gnw1_ref, gnw2_ref), parts, spots):
+                    for j in range(D // 128):
+                        at = o + j * up16(p)
+                        pack_ref[c, b, at:at + p, :] = g_ref[pl.ds(pl.multiple_of(d * p, p), p),
+                                                             128 * j:128 * j + 128].astype(BF)
+
+        for d in range(2 * bands):
+            g = d // group
+            pack_ref[d % 2, d // 2, tail:tail + 16, :] = jnp.concatenate(
+                [gvec_ref[:, 128 * g:128 * g + 128]] * 2, axis=0).astype(BF)
+
+
+def core(bands, parts, count, sid, rid, e, cot, snd, node, ncot, w1, w2, nw1, nw2, vec, R=512):
     E, D = e.shape
     nb = E // R
     S, N = snd.shape[0], node.shape[0]
@@ -180,52 +607,59 @@
     bb = pl.BlockSpec((R, D), lambda i: (jnp.maximum(i - nb, 0), 0))
     both = pl.BlockSpec((R, D), lambda i: (lax.rem(i, nb), 0))
     sds = jax.ShapeDtypeStruct
-    return pl.pallas_call(
-        functools.partial(kernel, nb, R),
+    slots = S // (2 * bands)
+    fast = all(p % 16 == 0 for p in parts)
+    rows = layout(parts)[1] + 16
+    grads = [(3 * D, D), (D, D), (2 * D, D), (D, D), (8, D)]
+    outs = [sds((N, D), BF), sds((E, D), BF), sds((N, D), F32), sds((E, D), F32),
+            sds((2 * bands, 2 * slots, D // 2), BF)]
+    outs += [sds((2, bands, rows, 128), BF)] if fast else [sds(g, F32) for g in grads]
+    *res, packed = res = pl.pallas_call(
+        functools.partial(core_kernel, nb, R, parts),
         grid=(2 * nb,),
         in_specs=[pl.BlockSpec(memory_space=pltpu.SMEM), V, V, both, bb, V, V, V, V, V, V, V, V],
-        out_specs=[V, fb, V, bb, V, V, V, V, V, V],
-        out_shape=[sds((N, D), BF), sds((E, D), BF), sds((N, D), F32), sds((E, D), F32),
-                   sds((3 * D, D), F32), sds((D, D), F32), sds((2 * D, D), F32), sds((D, D), F32),
-                   sds((8, D), F32), sds((S, D), BF)],
-        scratch_shapes=[pltpu.VMEM((D + S + N, D), BF), pltpu.VMEM((D, D), BF),
-                        pltpu.VMEM((E, D), BF), pltpu.VMEM((E, D), BF), pltpu.VMEM((E, D), BF),
-                        pltpu.VMEM((E, 128), F32), pltpu.VMEM((N, D), F32), pltpu.VMEM((N, D), BF),
-                        pltpu.VMEM((D + S + N, D), F32), pltpu.VMEM((8, D), F32), pltpu.VMEM((8, D), F32)],
+        out_specs=[V, fb, V, bb] + [V] * (len(outs) - 4),
+        out_shape=outs,
+        scratch_shapes=([pltpu.VMEM(g, F32) for g in grads] if fast else []) + [
+            pltpu.VMEM((D + S + N, D), BF), pltpu.VMEM((D, D), BF),
+            pltpu.VMEM((E, D), BF), pltpu.VMEM((E, D), BF), pltpu.VMEM((E, D), BF),
+            pltpu.VMEM((E, 128), F32), pltpu.VMEM((N, D), F32), pltpu.VMEM((N, D), BF),
+            pltpu.VMEM((D + S + N, D), F32), pltpu.VMEM((8, D), F32), pltpu.VMEM((8, D), F32)],
         compiler_params=pltpu.CompilerParams(vmem_limit_bytes=63 * 1024 * 1024, dimension_semantics=("arbitrary",)),
         name="edge_node_core",
     )(count, sid.reshape(nb, R), rid.reshape(nb, R), e, cot, snd, node, ncot, w1, w2, nw1, nw2, vec)
-
-
-AXES = ("band", "sub")
-
-
-def local(node_state, edge_state, send_rows, edge_sender, edge_receiver, edge_count, edge_w1, edge_b1, edge_w2,
+    if not fast:
+        packed = pack_grads(bands, parts, res[5:])
+    return (*res[:4], packed, res[4])
+
+
+def pack_grads(bands, parts, grads):
+    *mats, vec = [g.astype(BF) for g in grads]
+    n, D = 2 * bands, vec.shape[1]
+    blocks = []
+    for m, p in zip(mats, parts):
+        for j in range(D // 128):
+            block = m[:, 128 * j:128 * j + 128].reshape(n, p, 128)
+            blocks.append(jnp.pad(block, ((0, 0), (0, up16(p) - p), (0, 0))))
+    slabs = jnp.repeat(vec.reshape(8, D // 128, 128).transpose(1, 0, 2), n // (D // 128), axis=0)
+    full = jnp.concatenate(blocks + [slabs, slabs], axis=1)
+    return full.reshape(bands, 2, full.shape[1], 128).transpose(1, 0, 2, 3)
+
+
+def local(bands, node_state, edge_state, send_rows, edge_sender, edge_receiver, edge_count, edge_w1, edge_b1, edge_w2,
           edge_gain, edge_shift, node_w1, node_b1, node_w2, node_gain, node_shift, node_cot, edge_cot):
-    D = node_state.shape[1]
-    N = node_state.shape[0]
-    peers, slots = send_rows.shape[1:]
-    mats = (edge_w1, edge_w2, node_w1, node_w2)
+    parts = tuple(m.shape[0] for m in (edge_w1, edge_w2, node_w1, node_w2))
+    width = edge_b1.shape[0]
     vecs = (edge_b1, edge_gain, edge_shift, node_b1, node_gain, node_shift)
-    part = vecs[0].shape[0]
-    w1, w2, nw1, nw2 = (lax.all_gather(m, AXES, axis=0, tiled=True) for m in mats)
-    vec = lax.all_gather(jnp.stack(vecs), AXES, axis=1, tiled=True)
-    vec = jnp.concatenate([vec, jnp.zeros((2, D), BF)], axis=0)
-    selected = send_rows[0].reshape(peers * slots)
-    outgoing = jnp.take(node_state, selected, axis=0).reshape(peers, slots, D)
-    senders = lax.all_to_all(outgoing, AXES, split_axis=0, concat_axis=0, tiled=True).reshape(peers * slots, D)
-    node_out, edge_out, node_grad, edge_grad, gw1, gw2, gnw1, gnw2, gvec, sgrad = core(
-        edge_count, edge_sender, edge_receiver, edge_state, edge_cot, senders, node_state, node_cot,
+    sel = send_rows[0]
+    none = jnp.zeros((width,), BF)
+    w1, w2, nw1, nw2, vec, senders = gather_weights(
+        bands, edge_w1, edge_w2, node_w1, node_w2, jnp.stack(vecs + (none, none)), sel, node_state)
+    node_out, edge_out, node_part, edge_grad, packed, msgs = core(
+        bands, parts, edge_count, edge_sender, edge_receiver, edge_state, edge_cot, senders, node_state, node_cot,
         w1, w2, nw1, nw2, vec)
-    arrived = lax.all_to_all(sgrad.reshape(peers, slots, D), AXES, split_axis=0, concat_axis=0, tiled=True)
-    node_grad = node_grad + jax.ops.segment_sum(
-        arrived.reshape(peers * slots, D).astype(F32), selected, num_segments=N)
-
-    def scatter(v):
-        return lax.psum_scatter(v, AXES, scatter_dimension=0, tiled=True)
-
-    gw1, gw2, gnw1, gnw2 = (scatter(v) for v in (gw1, gw2, gnw1, gnw2))
-    gv = lax.psum_scatter(gvec, AXES, scatter_dimension=1, tiled=True)
+    red, arrived = reduce_grads(bands, packed, msgs)
+    node_grad, gw1, gw2, gnw1, gnw2, *gv = finish(bands, parts, width, red, arrived, sel, node_part)
     return (node_out, edge_out, node_grad, edge_grad, gw1, gv[0], gw2, gv[1], gv[2], gnw1, gv[3], gnw2, gv[4], gv[5])
 
 
@@ -233,4 +667,5 @@
     two, one, three = P(AXES, None), P(AXES), P(AXES, None, None)
     in_specs = (two, two, three, one, one, one, two, one, two, one, one, two, one, two, one, one, two, two)
     out_specs = (two, two, two, two, two, one, two, one, one, two, one, two, one, one)
-    return jax.shard_map(local, mesh=mesh, in_specs=in_specs, out_specs=out_specs, check_vma=False)
+    return jax.shard_map(functools.partial(local, mesh.shape["band"]), mesh=mesh, in_specs=in_specs,
+                         out_specs=out_specs, check_vma=False)

time: 890 us -> 171 us (0.19)
  waiting for transfers between devices: 631 us -> 0 us
  blocking collectives: 126 us -> 0 us
  Pallas kernels: 88.6 us -> 162 us
  between operations: 14.9 us -> 1.32 us
  starting transfers between devices: 10.2 us -> 0 us
  local copies, waits for them, and re-layouts: 14.4 us -> 5.45 us
    reduce_scatter x4 -> x0, waiting for transfers between devices: 502 us -> none  [scatter(): return lax.psum_scatter(v, AXES, scatter_dimension=0, tiled=True)]
    unnamed x8 -> x0, waiting for transfers between devices: 129 us -> none
    all_gather x3 -> x0, blocking collectives: 126 us -> none  [the longest x2 83.7 us: local(): lax.all_gather(m, AXES, axis=0, tiled=True)]
    pallas_call x1 -> x4, Pallas kernels: 88.6 us -> 162 us  [the longest x1 87.7 us: core(): pl.pallas_call(functools.partial(core_kernel, nb, R, parts), grid=(2 * nb...]
    all_to_all x2 -> x0, starting transfers between devices: 9.9 us -> none  [the longest x1 7.3 us: local(): lax.all_to_all(outgoing, AXES, split_axis=0, concat_axis=0, tiled=True)]
  transfers between devices with their start and end apart: 9 -> 0, of which waited for: 5 -> 0; matrix products, arithmetic and copies ran while one was open for 2% -> 0% of each run, Pallas kernels for 0% -> 0%
where the time goes in v2:
time: 171 us; the launch traced here: 169 us
  Pallas kernels  162 us (95%)
  local copies, waits for them, and re-layouts  5.45 us (3%)
    pallas_call x1, Pallas kernels, core(): pl.pallas_call(functools.partial(core_kernel, nb, R, parts), grid=(2 * nb...  87.7 us
    pallas_call x1, Pallas kernels, reduce_grads(): pl.pallas_call(functools.partial(reduce_kernel, bands), out_shape=[sds((r...  35.8 us
    pallas_call x1, Pallas kernels, gather_weights(): pl.pallas_call(functools.partial(gather_kernel, bands, parts, fast), out_...  35.4 us

profile of v2, /device:TPU:0, one launch (start us, length us, event | category | flops | bytes accessed | tf_op | source)
XLA Modules:
  0.0 168.8 jit_solution(15706920023221387068)
XLA Ops:
  1.3 1.3 stack.31.vec_ref
  2.6 1.4 copy.32
  4.0 1.4 reshape.34.sid_ref
  5.4 1.4 reshape.35.rid_ref
  6.8 35.4 %gather_weights.1 = (bf16[1536,512]{1,0:T(8,128)(2,1)}, bf16[512,512]{1,0:T(8,128)(2,1)}, bf16[1024,512]{1,0:T(8,128)(2,1)}, bf16[512,512]{1,0:T(8,128)(2,1)}, b...) custom-call(bf16[48,512]{1,0:T(8,128)(2,1)} %w1_ref.1, bf16[16,512]{1,0:T(8,128)(2,1)} %w2_ref.1, ...), custom_call_target="tpu_custom_call" | custom-call | tf_op jit(solution)/shard_map/gather_weights/pallas_call | solution.py:213
  42.2 87.7 %edge_node_core.1 = (bf16[512,512]{1,0:T(8,128)(2,1)}, bf16[8192,512]{1,0:T(8,128)(2,1)}, f32[512,512]{1,0:T(8,128)}, f32[8192,512]{1,0:T(8,128)}, bf16[32,16,25...) custom-call(s32[1]{0:T(128)S(6)} %copy.33.count_ref, s32[16,512]{1,0:T(8,128)} %reshape.34.sid_ref, ...), custom_call_target="tpu_custom_call" | custom-call | tf_op jit(solution)/shard_map/edge_node_core/pallas_call | solution.py:617
  129.8 35.8 %reduce_grads.1 = (f32[464,128]{1,0:T(8,128)}, bf16[32,16,256]{2,1,0:T(8,128)(2,1)}) custom-call(bf16[2,16,464,128]{3,2,1,0:T(8,128)(2,1)} %get-tuple-element.47.p_ref, bf16[32,16,256]{2,1,0:T(8,128)(2,1)} %get-tuple-element.48.msg_ref), custom_call_target="tpu_custom_call" | custom-call | tf_op jit(solution)/shard_map/reduce_grads/pallas_call | solution.py:348
  165.7 3.2 %finish.1 = (f32[512,512]{1,0:T(8,128)}, f32[48,512]{1,0:T(8,128)}, f32[16,512]{1,0:T(8,128)}, f32[32,512]{1,0:T(8,128)}, f32[16,512]{1,0:T(8,128)}, /*index=5*/...) custom-call(f32[464,128]{1,0:T(8,128)} %get-tuple-element.49.red_ref, ...), custom_call_target="tpu_custom_call" | custom-call | tf_op jit(solution)/shard_map/finish/pallas_call | solution.py:404
  (1 shorter events, 0.0 us)

commit v3 on v2

--- a/solution.py
+++ b/solution.py
@@ -58,11 +58,12 @@
     pl.semaphore_wait(sem, pos.devices - 1)
 
 
-def gather_kernel(bands, parts, fast, w1_ref, w2_ref, nw1_ref, nw2_ref, vec_ref, sel_ref, node_ref, *refs):
+def gather_kernel(bands, parts, fast, w1_ref, w2_ref, nw1_ref, nw2_ref, sel_ref, node_ref, *refs):
+    vecs, refs = refs[:6], refs[6:]
     if fast:
-        outs, (vec_out, snd_out, buf, outg, inc, recv, half, send, a_recv, a_send) = refs[:4], refs[4:]
+        outs, (vec_out, snd_out, buf, wide, outg, inc, recv, half, send, a_recv, a_send) = refs[:4], refs[4:]
     else:
-        (buf, vec_out, snd_out, outg, inc, recv, half, send, a_recv, a_send) = refs
+        (buf, vec_out, snd_out, wide, outg, inc, recv, half, send, a_recv, a_send) = refs
         outs = None
     pos = Place(bands)
     spots, tail = layout(parts)
@@ -71,16 +72,21 @@
     me, c, a, q = pos.me, pos.c, pos.a, pos.q
     mats = (w1_ref, w2_ref, nw1_ref, nw2_ref)
     D = node_ref.shape[1]
-    peers, slots = sel_ref.shape
+    slots, peers = sel_ref.shape
     S = peers * slots
     for m, p, o in zip(mats, parts, spots):
         for j in range(4):
             buf[me, o + j * up16(p):o + j * up16(p) + p, :] = m[:, 128 * j:128 * j + 128]
-    group = 128 // vec_ref.shape[1]
-    lanes = lax.broadcasted_iota(jnp.int32, (8, 128), 1)
-    vals = jnp.concatenate([vec_ref[...]] * group, axis=1).astype(F32)
-    vals = jnp.where(lanes // vec_ref.shape[1] == me % group, vals, 0.0)
-    buf[me, tail:tail + 16, :] = jnp.concatenate([vals, jnp.zeros((8, 128), F32)], axis=0).astype(BF)
+    width = vecs[0].shape[0]
+    group = 128 // width
+    lanes = lax.broadcasted_iota(jnp.int32, (1, 128), 1)
+    for k in range(16):
+        if k < 6:
+            val = jnp.concatenate([vecs[k][...].astype(F32).reshape(1, width)] * group, axis=1)
+            wide[k:k + 1, :] = jnp.where(lanes // width == me % group, val, 0.0)
+        else:
+            wide[k:k + 1, :] = jnp.zeros((1, 128), F32)
+    buf[me, tail:tail + 16, :] = wide[...].astype(BF)
     barrier_all(pos)
     count = [0]
 
@@ -120,14 +126,7 @@
 
     spread(me)
     sibling(me)
-    ids = sel_ref[...]
-    pick = (lax.broadcasted_iota(jnp.int32, (S, peers), 0) // slots
-            == lax.broadcasted_iota(jnp.int32, (S, peers), 1)).astype(BF)
-    low = jnp.dot(pick, (ids % 256).astype(BF), preferred_element_type=F32)
-    high = jnp.dot(pick, (ids // 256).astype(BF), preferred_element_type=F32)
-    mine = lax.broadcasted_iota(jnp.int32, (S, slots), 0) % slots == lax.broadcasted_iota(jnp.int32, (S, slots), 1)
-    col = jnp.sum(jnp.where(mine, low + 256.0 * high, 0.0), axis=1, keepdims=True)
-    hot = (col == lax.broadcasted_iota(jnp.int32, (S, node_ref.shape[0]), 1).astype(F32)).astype(BF)
+    hot = slot_onehot(sel_ref[...], node_ref.shape[0])
     picked = jnp.dot(hot, node_ref[...], preferred_element_type=F32)
     outg[:, 0:slots, :] = picked[:, 0:D // 2].reshape(peers, slots, D // 2).astype(BF)
     outg[:, slots:, :] = picked[:, D // 2:].reshape(peers, slots, D // 2).astype(BF)
@@ -190,7 +189,7 @@
         cp.wait_send()
 
 
-def gather_weights(bands, w1, w2, nw1, nw2, vec, sel, node):
+def gather_weights(bands, w1, w2, nw1, nw2, sel, node, *vecs):
     parts = tuple(m.shape[0] for m in (w1, w2, nw1, nw2))
     fast = all(p % 16 == 0 for p in parts)
     _, tail = layout(parts)
@@ -198,7 +197,7 @@
     n = bands * 2
     quads = bands // LINE
     D = node.shape[1]
-    peers, slots = sel.shape
+    slots, peers = sel.shape
     S = peers * slots
     V = pl.BlockSpec(memory_space=pltpu.VMEM)
     sds = jax.ShapeDtypeStruct
@@ -207,15 +206,16 @@
     outs = (full if fast else [shards]) + [sds((16, D), BF), sds((S, D), BF)]
     sends = (quads - 1) + 2 * quads + 2 * quads + 4 * quads
     scratch = ([pltpu.VMEM(shards.shape, BF)] if fast else []) + [
+        pltpu.VMEM((16, 128), F32),
         pltpu.VMEM((peers, 2 * slots, D // 2), BF), pltpu.VMEM((peers, 2 * slots, D // 2), BF),
         pltpu.SemaphoreType.DMA((n,)), pltpu.SemaphoreType.DMA((2, quads)), pltpu.SemaphoreType.DMA((sends,)),
         pltpu.SemaphoreType.DMA((n,)), pltpu.SemaphoreType.DMA((n,))]
     res = pl.pallas_call(
         functools.partial(gather_kernel, bands, parts, fast),
-        out_shape=outs, in_specs=[V] * 7, out_specs=[V] * len(outs), scratch_shapes=scratch,
+        out_shape=outs, in_specs=[V] * 12, out_specs=[V] * len(outs), scratch_shapes=scratch,
         compiler_params=pltpu.CompilerParams(collective_id=0, has_side_effects=True, vmem_limit_bytes=60 * 2**20),
         name="gather_weights",
-    )(w1, w2, nw1, nw2, vec, sel, node)
+    )(w1, w2, nw1, nw2, sel, node, *vecs)
     if fast:
         return res
     got, vec, snd = res
@@ -375,7 +375,7 @@
         got = jnp.where(me % group == g, slab[:, g * width:(g + 1) * width], got)
     for k, v_ref in enumerate(vecs):
         v_ref[...] = got[k]
-    peers, slots = sel_ref.shape
+    slots, peers = sel_ref.shape
     S = peers * slots
     N, D = part_ref.shape
     hot = slot_onehot(sel_ref[...], N)
@@ -385,12 +385,12 @@
 
 
 def slot_onehot(ids, nodes):
-    peers, slots = ids.shape
+    slots, peers = ids.shape
     S = peers * slots
     pick = (lax.broadcasted_iota(jnp.int32, (S, peers), 0) // slots
             == lax.broadcasted_iota(jnp.int32, (S, peers), 1)).astype(BF)
-    low = jnp.dot(pick, (ids % 256).astype(BF), preferred_element_type=F32)
-    high = jnp.dot(pick, (ids // 256).astype(BF), preferred_element_type=F32)
+    low = dot_t(pick, (ids % 256).astype(BF))
+    high = dot_t(pick, (ids // 256).astype(BF))
     mine = lax.broadcasted_iota(jnp.int32, (S, slots), 0) % slots == lax.broadcasted_iota(jnp.int32, (S, slots), 1)
     col = jnp.sum(jnp.where(mine, low + 256.0 * high, 0.0), axis=1, keepdims=True)
     return (col == lax.broadcasted_iota(jnp.int32, (S, nodes), 1).astype(F32)).astype(BF)
@@ -411,97 +411,145 @@
 
 EPS = 1e-5
 
+
 def dot(a, b):
     return jnp.dot(a, b, preferred_element_type=F32)
 
+
 def dot_t(a, b):
     return lax.dot_general(a, b, (((1,), (1,)), ((), ())), preferred_element_type=F32)
 
+
 def t_dot(a, b):
     return lax.dot_general(a, b, (((0,), (0,)), ((), ())), preferred_element_type=F32)
 
+
 def rowmean(v):
     return jnp.sum(v, axis=1, keepdims=True) * (1.0 / v.shape[1])
 
-def norm(v):
-    c = v - rowmean(v)
-    s = lax.rsqrt(rowmean(c * c) + EPS)
-    return c * s, s
-
-def core_kernel(nb, R, parts, count_ref, sid_ref, rid_ref, e_ref, cot_ref, snd_ref, node_ref, ncot_ref,
-           w1_ref, w2_ref, nw1_ref, nw2_ref, vec_ref,
-           nout_ref, eout_ref, ngrad_ref, egrad_ref, msg_ref, *refs):
-    fast = all(p % 16 == 0 for p in parts)
-    pack_ref = refs[0] if fast else None
-    (gw1_ref, gw2_ref, gnw1_ref, gnw2_ref, gvec_ref, wcat, w2h, hid_s, slope_s, nrm_s, scale_s, gath, dg, gacc, gain_acc, shift_acc) = refs[fast:]
+
+def onehot_cols(ids, width):
+    rows = ids.shape[1]
+    wide = jnp.broadcast_to(ids, (128, rows)).T
+    off = wide - lax.broadcasted_iota(jnp.int32, (rows, 128), 1)
+    return jnp.concatenate([jnp.where(off == 128 * j, 1.0, 0.0).astype(BF) for j in range(width // 128)], axis=1)
+
+
+def onehot_rows(ids, height):
+    return jnp.where(lax.broadcasted_iota(jnp.int32, (height, ids.shape[1]), 0) == ids, 1.0, 0.0).astype(BF)
+
+
+def fold8(v):
+    return jnp.sum(v.reshape(v.shape[0] // 8, 8, v.shape[1]), axis=0)
+
+
+def core_kernel(nb, R, sub, parts, fast, count_ref, sid_ref, rid_ref, e_ref, cot_ref, snd_ref, node_ref, ncot_ref,
+                w1_ref, w2_ref, nw1_ref, nw2_ref, vec_ref,
+                nout_ref, eout_ref, ngrad_ref, egrad_ref, msg_ref, *refs):
+    outs, refs = (refs[:1], refs[1:]) if fast else (refs[:5], refs[5:])
+    wcat, w2h, hid_s, slope_s, nrm_s, scale_s, gath, dg, gacc, g2acc, gain_acc, shift_acc, gvec, msg_s, dpre_s, w1t = refs
     i = pl.program_id(0)
     D = e_ref.shape[1]
     S = snd_ref.shape[0]
     N = node_ref.shape[0]
     count = count_ref[0]
-    b1 = vec_ref[0:1, :].astype(F32)
     gain = vec_ref[1:2, :].astype(F32)
     shift = vec_ref[2:3, :].astype(F32)
+    spots, tail = layout(parts)
+    n = 3 * D // parts[0]
+
+    def emit(m, first, value):
+        if not fast:
+            outs[m][first:first + value.shape[0], :] = value
+            return
+        p, o = parts[m], spots[m]
+        lo, hi = first, first + value.shape[0]
+        for d in range(lo // p, -(-hi // p)):
+            a, b = max(lo, d * p), min(hi, (d + 1) * p)
+            for j in range(D // 128):
+                at = o + j * p + a - d * p
+                outs[0][d % 2, d // 2, at:at + b - a, :] = value[a - lo:b - lo, 128 * j:128 * j + 128].astype(BF)
 
     @pl.when(i == 0)
     def _():
+        b1 = vec_ref[0:1, :].astype(F32)
         wcat[0:D, :] = w1_ref[0:D, :] * 0.5
         wcat[D:D + S, :] = (dot(snd_ref[...], w1_ref[D:2 * D, :]) * 0.5).astype(BF)
         wcat[D + S:, :] = ((dot(node_ref[...], w1_ref[2 * D:, :]) + b1) * 0.5).astype(BF)
-        w2h[...] = w2_ref[...] * 0.5
+        w2h[...] = (w2_ref[...].astype(F32) * 0.5).T.astype(BF)
+        w1t[...] = w1_ref[0:D, :].astype(F32).T.astype(BF)
         gath[...] = jnp.zeros_like(gath)
         gacc[...] = jnp.zeros_like(gacc)
-        gw2_ref[...] = jnp.zeros_like(gw2_ref)
+        g2acc[...] = jnp.zeros_like(g2acc)
         gain_acc[...] = jnp.zeros_like(gain_acc)
         shift_acc[...] = jnp.zeros_like(shift_acc)
+        scale_s[...] = jnp.zeros_like(scale_s)
 
     blk = lax.rem(i, nb)
-    first = blk * R
-    rows = pl.ds(pl.multiple_of(first, R), R)
-    live_blk = first < count
-
-    def onehot_cols(ids_row, width):
-        ids = jnp.broadcast_to(ids_row, (128, R)).T
-        lane = lax.broadcasted_iota(jnp.int32, (R, 128), 1)
-        d = ids - lane
-        parts = [jnp.where(d == 128 * j, 1.0, 0.0).astype(BF) for j in range(width // 128)]
-        return jnp.concatenate(parts, axis=1)
-
-    def onehot_rows(ids_row, height):
-        sub = lax.broadcasted_iota(jnp.int32, (height, R), 0)
-        return jnp.where(sub == ids_row, 1.0, 0.0).astype(BF)
-
-    def ids():
-        pos = first + lax.broadcasted_iota(jnp.int32, (1, R), 1)
-        sid = sid_ref[pl.ds(blk, 1), :]
-        rid = jnp.where(pos < count, rid_ref[pl.ds(blk, 1), :], -1)
+    live_blk = blk * R < count
+    subs = R // sub
+
+    def ids(r):
+        at = blk * subs + r
+        pos = at * sub + lax.broadcasted_iota(jnp.int32, (1, sub), 1)
+        sid = sid_ref[pl.ds(at, 1), :]
+        rid = jnp.where(pos < count, rid_ref[pl.ds(at, 1), :], -1)
         return sid, rid
 
-    def live_col():
-        return first + lax.broadcasted_iota(jnp.int32, (R, 1), 0) < count
+    def live_col(r):
+        return (blk * subs + r) * sub + lax.broadcasted_iota(jnp.int32, (sub, 1), 0) < count
+
+    def lane_is(at):
+        return lax.broadcasted_iota(jnp.int32, (sub, 128), 1) == at
 
     @pl.when((i < nb) & live_blk)
     def _():
-        sid, rid = ids()
-        x = jnp.concatenate([e_ref[...], onehot_cols(sid, S), onehot_cols(rid, N)], axis=1)
-        h = dot(x, wcat[...])
-        a = 1.0 + jnp.tanh(h)
-        hid = h * a
-        slope = a * (1.0 + 2.0 * h - hid)
-        hid = hid.astype(BF)
-        hid_s[rows, :] = hid
-        slope_s[rows, :] = slope.astype(BF)
-        proj = dot(hid, w2_ref[...])
-        live = live_col()
-        c = proj - rowmean(proj)
-        s = lax.rsqrt(rowmean(c * c) + EPS)
-        s = jnp.where(live, s, 0.0)
-        scale_s[rows, :] = jnp.broadcast_to(s, (R, 128))
-        nrm = c * s
-        nrm_s[rows, :] = nrm.astype(BF)
-        msg = nrm * gain + shift
-        eout_ref[...] = (e_ref[...].astype(F32) + jnp.where(live, msg, 0.0)).astype(BF)
-        gath[...] += dot(onehot_rows(rid, N), msg.astype(BF))
+        here = [slice(r * sub, (r + 1) * sub) for r in range(subs)]
+        rows = [pl.ds(pl.multiple_of((blk * subs + r) * sub, sub), sub) for r in range(subs)]
+        idx = [ids(r) for r in range(subs)]
+        h, proj = [None] * subs, [None] * subs
+
+        def a1(r):
+            sid, rid = idx[r]
+            x = jnp.concatenate([e_ref[here[r], :], onehot_cols(sid, S), onehot_cols(rid, N)], axis=1)
+            h[r] = dot(x, wcat[...])
+
+        def a2(r):
+            v = h[r]
+            a = 1.0 + jnp.tanh(v)
+            hid = v * a
+            slope_s[rows[r], :] = (a * (1.0 + 2.0 * v - hid)).astype(BF)
+            hid_s[rows[r], :] = hid.astype(BF)
+
+        def b1(r):
+            proj[r] = dot(hid_s[rows[r], :], w2_ref[...])
+
+        def b2(r):
+            live = live_col(r)
+            c = proj[r] - rowmean(proj[r])
+            s = lax.rsqrt(rowmean(c * c) + EPS)
+            s = jnp.where(live, s, 0.0)
+            scale_s[...] = jnp.where(lane_is(blk * subs + r), s, scale_s[...])
+            nrm = c * s
+            nrm_s[rows[r], :] = nrm.astype(BF)
+            msg = nrm * gain + shift
+            eout_ref[here[r], :] = (e_ref[here[r], :].astype(F32) + jnp.where(live, msg, 0.0)).astype(BF)
+            msg_s[here[r], :] = msg.astype(BF)
+
+        def c1(first, last):
+            rid = jnp.concatenate([idx[r][1] for r in range(first, last)], axis=1)
+            gath[...] += dot(onehot_rows(rid, N), msg_s[first * sub:last * sub, :])
+
+        for t in range(subs + 2):
+            if t < subs:
+                a1(t)
+            if 2 <= t:
+                b2(t - 2)
+            if 1 <= t < subs + 1:
+                b1(t - 1)
+            if t < subs:
+                a2(t)
+        c1(0, subs)
 
     @pl.when((i < nb) & jnp.logical_not(live_blk))
     def _():
@@ -518,43 +566,78 @@
         sig = 0.5 + 0.5 * jnp.tanh(0.5 * pre)
         hid = (pre * sig).astype(BF)
         proj = dot(hid, nw2_ref[...])
-        nrm, s = norm(proj)
+        c = proj - rowmean(proj)
+        s = lax.rsqrt(rowmean(c * c) + EPS)
+        nrm = c * s
         nout_ref[...] = (node.astype(F32) + nrm * ngain + nshift).astype(BF)
         up = ncot_ref[...].astype(F32)
-        gvec_ref[4:5, :] = jnp.sum(up * nrm, axis=0, keepdims=True)
-        gvec_ref[5:6, :] = jnp.sum(up, axis=0, keepdims=True)
+        gvec[4:5, :] = jnp.sum(up * nrm, axis=0, keepdims=True)
+        gvec[5:6, :] = jnp.sum(up, axis=0, keepdims=True)
         g = up * ngain
         dproj = (s * (g - rowmean(g) - nrm * rowmean(g * nrm))).astype(BF)
-        gnw2_ref[...] = t_dot(hid, dproj)
+        emit(3, 0, t_dot(hid, dproj))
         dpre = dot_t(dproj, nw2_ref[...]) * (sig * (1.0 + pre * (1.0 - sig)))
         dpre16 = dpre.astype(BF)
-        gnw1_ref[0:D, :] = t_dot(node, dpre16)
-        gnw1_ref[D:, :] = t_dot(g16, dpre16)
-        gvec_ref[3:4, :] = jnp.sum(dpre16.astype(F32), axis=0, keepdims=True)
+        emit(2, 0, t_dot(node, dpre16))
+        emit(2, D, t_dot(g16, dpre16))
+        gvec[3:4, :] = jnp.sum(dpre16.astype(F32), axis=0, keepdims=True)
         ngrad_ref[...] = up + dot_t(dpre16, nw1_ref[0:D, :])
         dg[...] = dot_t(dpre16, nw1_ref[D:, :]).astype(BF)
 
     @pl.when((i >= nb) & live_blk)
     def _():
-        sid, rid = ids()
-        live = live_col()
-        cot = cot_ref[...].astype(F32)
-        dm = jnp.where(live, cot, 0.0) + dot(onehot_cols(rid, N), dg[...])
-        nrm = nrm_s[rows, :].astype(F32)
-        p = dm * nrm
-        gain_acc[...] += jnp.sum(p.reshape(R // 8, 8, D), axis=0)
-        shift_acc[...] += jnp.sum(dm.reshape(R // 8, 8, D), axis=0)
-        g = dm * gain
-        m1 = rowmean(g)
-        m2 = rowmean(p * gain)
-        s = scale_s[rows, 0:1]
-        dproj = (s * (g - m1 - nrm * m2)).astype(BF)
-        gw2_ref[...] += t_dot(hid_s[rows, :], dproj)
-        dpre = (dot_t(dproj, w2h[...]) * slope_s[rows, :].astype(F32)).astype(BF)
-        gacc[0:D, :] += t_dot(e_ref[...], dpre)
-        gacc[D:D + S, :] += dot(onehot_rows(sid, S), dpre)
-        gacc[D + S:, :] += dot(onehot_rows(rid, N), dpre)
-        egrad_ref[...] = cot + dot_t(dpre, w1_ref[0:D, :])
+        here = [slice(r * sub, (r + 1) * sub) for r in range(subs)]
+        rows = [pl.ds(pl.multiple_of((blk * subs + r) * sub, sub), sub) for r in range(subs)]
+        every = pl.ds(pl.multiple_of(blk * R, R), R)
+        idx = [ids(r) for r in range(subs)]
+        came, dhid, back = [None] * subs, [None] * subs, [None] * subs
+
+        def a1(r):
+            came[r] = dot(onehot_cols(idx[r][1], N), dg[...])
+
+        def a2(r):
+            dm = jnp.where(live_col(r), cot_ref[here[r], :].astype(F32), 0.0) + came[r]
+            nrm = nrm_s[rows[r], :].astype(F32)
+            p = dm * nrm
+            gain_acc[...] += fold8(p)
+            shift_acc[...] += fold8(dm)
+            g = dm * gain
+            m1 = rowmean(g)
+            m2 = rowmean(p * gain)
+            s = jnp.sum(jnp.where(lane_is(blk * subs + r), scale_s[...], 0.0), axis=1, keepdims=True)
+            msg_s[here[r], :] = (s * (g - m1 - nrm * m2)).astype(BF)
+
+        def b1(r):
+            dhid[r] = dot(msg_s[here[r], :], w2h[...])
+
+        def b2(r):
+            dpre_s[here[r], :] = (dhid[r] * slope_s[rows[r], :].astype(F32)).astype(BF)
+
+        def c1(r):
+            back[r] = dot(dpre_s[here[r], :], w1t[...])
+
+        def c2(r):
+            egrad_ref[here[r], :] = cot_ref[here[r], :].astype(F32) + back[r]
+
+        for t in range(subs + 3):
+            if t < subs:
+                a1(t)
+            if t >= 3:
+                c2(t - 3)
+            if 2 <= t < subs + 2:
+                b2(t - 2)
+            if 1 <= t < subs + 1:
+                b1(t - 1)
+            if t < subs:
+                a2(t)
+            if 2 <= t < subs + 2:
+                c1(t - 2)
+        g2acc[...] += t_dot(hid_s[every, :], msg_s[...])
+        sids = jnp.concatenate([v[0] for v in idx], axis=1)
+        rids = jnp.concatenate([v[1] for v in idx], axis=1)
+        gacc[0:D, :] += t_dot(e_ref[...], dpre_s[...])
+        gacc[D:D + S, :] += dot(onehot_rows(sids, S), dpre_s[...])
+        gacc[D + S:, :] += dot(onehot_rows(rids, N), dpre_s[...])
 
     @pl.when((i >= nb) & jnp.logical_not(live_blk))
     def _():
@@ -562,44 +645,33 @@
 
     @pl.when(i == 2 * nb - 1)
     def _():
-        gvec_ref[1:2, :] = jnp.sum(gain_acc[...], axis=0, keepdims=True)
-        gvec_ref[2:3, :] = jnp.sum(shift_acc[...], axis=0, keepdims=True)
-        gvec_ref[0:1, :] = jnp.sum(gacc[D + S:, :], axis=0, keepdims=True)
-        gvec_ref[6:8, :] = jnp.zeros((2, D), F32)
         us = gacc[D:D + S, :].astype(BF)
         ur = gacc[D + S:, :].astype(BF)
-        gw1_ref[0:D, :] = gacc[0:D, :]
-        gw1_ref[D:2 * D, :] = t_dot(snd_ref[...], us)
-        gw1_ref[2 * D:, :] = t_dot(node_ref[...], ur)
+        emit(0, 0, gacc[0:D, :])
+        emit(0, D, t_dot(snd_ref[...], us))
+        emit(0, 2 * D, t_dot(node_ref[...], ur))
+        emit(1, 0, g2acc[...])
+        ngrad_ref[...] += dot_t(ur, w1_ref[2 * D:, :])
         sgrad = dot_t(us, w1_ref[D:2 * D, :])
         peers, slots = msg_ref.shape[0], msg_ref.shape[1] // 2
         msg_ref[:, 0:slots, :] = sgrad[:, 0:D // 2].reshape(peers, slots, D // 2).astype(BF)
         msg_ref[:, slots:, :] = sgrad[:, D // 2:].reshape(peers, slots, D // 2).astype(BF)
-        ngrad_ref[...] += dot_t(ur, w1_ref[2 * D:, :])
+        gvec[0:1, :] = jnp.sum(gacc[D + S:, :], axis=0, keepdims=True)
+        gvec[1:2, :] = jnp.sum(gain_acc[...], axis=0, keepdims=True)
+        gvec[2:3, :] = jnp.sum(shift_acc[...], axis=0, keepdims=True)
+        gvec[6:8, :] = jnp.zeros((2, D), F32)
         if not fast:
-            return
-        spots, tail = layout(parts)
-        bands = pack_ref.shape[1]
-        group = 2 * bands // (D // 128)
-
-        @pl.loop(0, bands)
-        def _(b):
-            for c in range(2):
-                d = b * 2 + c
-                for g_ref, p, o in zip((gw1_ref, gw2_ref, gnw1_ref, gnw2_ref), parts, spots):
-                    for j in range(D // 128):
-                        at = o + j * up16(p)
-                        pack_ref[c, b, at:at + p, :] = g_ref[pl.ds(pl.multiple_of(d * p, p), p),
-                                                             128 * j:128 * j + 128].astype(BF)
-
-        for d in range(2 * bands):
-            g = d // group
-            pack_ref[d % 2, d // 2, tail:tail + 16, :] = jnp.concatenate(
-                [gvec_ref[:, 128 * g:128 * g + 128]] * 2, axis=0).astype(BF)
-
-
-def core(bands, parts, count, sid, rid, e, cot, snd, node, ncot, w1, w2, nw1, nw2, vec, R=512):
+            outs[4][...] = gvec[...]
+        else:
+            for d in range(n):
+                g = d * D // n // 128
+                outs[0][d % 2, d // 2, tail:tail + 16, :] = jnp.concatenate(
+                    [gvec[:, 128 * g:128 * g + 128]] * 2, axis=0).astype(BF)
+
+
+def core(bands, parts, count, sid, rid, e, cot, snd, node, ncot, w1, w2, nw1, nw2, vec, sub=128):
     E, D = e.shape
+    R = 1024 if snd.shape[0] <= 256 else 512
     nb = E // R
     S, N = snd.shape[0], node.shape[0]
     V = pl.BlockSpec(memory_space=pltpu.VMEM)
@@ -614,20 +686,20 @@
     outs = [sds((N, D), BF), sds((E, D), BF), sds((N, D), F32), sds((E, D), F32),
             sds((2 * bands, 2 * slots, D // 2), BF)]
     outs += [sds((2, bands, rows, 128), BF)] if fast else [sds(g, F32) for g in grads]
+    vm = pltpu.VMEM
     *res, packed = res = pl.pallas_call(
-        functools.partial(core_kernel, nb, R, parts),
+        functools.partial(core_kernel, nb, R, sub, parts, fast),
         grid=(2 * nb,),
         in_specs=[pl.BlockSpec(memory_space=pltpu.SMEM), V, V, both, bb, V, V, V, V, V, V, V, V],
         out_specs=[V, fb, V, bb] + [V] * (len(outs) - 4),
         out_shape=outs,
-        scratch_shapes=([pltpu.VMEM(g, F32) for g in grads] if fast else []) + [
-            pltpu.VMEM((D + S + N, D), BF), pltpu.VMEM((D, D), BF),
-            pltpu.VMEM((E, D), BF), pltpu.VMEM((E, D), BF), pltpu.VMEM((E, D), BF),
-            pltpu.VMEM((E, 128), F32), pltpu.VMEM((N, D), F32), pltpu.VMEM((N, D), BF),
-            pltpu.VMEM((D + S + N, D), F32), pltpu.VMEM((8, D), F32), pltpu.VMEM((8, D), F32)],
-        compiler_params=pltpu.CompilerParams(vmem_limit_bytes=63 * 1024 * 1024, dimension_semantics=("arbitrary",)),
+        scratch_shapes=[
+            vm((D + S + N, D), BF), vm((D, D), BF), vm((E, D), BF), vm((E, D), BF), vm((E, D), BF),
+            vm((sub, 128), F32), vm((N, D), F32), vm((N, D), BF), vm((D + S + N, D), F32), vm((D, D), F32),
+            vm((8, D), F32), vm((8, D), F32), vm((8, D), F32), vm((R, D), BF), vm((R, D), BF), vm((D, D), BF)],
+        compiler_params=pltpu.CompilerParams(vmem_limit_bytes=63 * 2**20, dimension_semantics=("arbitrary",)),
         name="edge_node_core",
-    )(count, sid.reshape(nb, R), rid.reshape(nb, R), e, cot, snd, node, ncot, w1, w2, nw1, nw2, vec)
+    )(count, sid.reshape(E // sub, sub), rid.reshape(E // sub, sub), e, cot, snd, node, ncot, w1, w2, nw1, nw2, vec)
     if not fast:
         packed = pack_grads(bands, parts, res[5:])
     return (*res[:4], packed, res[4])
@@ -651,10 +723,9 @@
     parts = tuple(m.shape[0] for m in (edge_w1, edge_w2, node_w1, node_w2))
     width = edge_b1.shape[0]
     vecs = (edge_b1, edge_gain, edge_shift, node_b1, node_gain, node_shift)
-    sel = send_rows[0]
-    none = jnp.zeros((width,), BF)
+    sel = send_rows[0].T
     w1, w2, nw1, nw2, vec, senders = gather_weights(
-        bands, edge_w1, edge_w2, node_w1, node_w2, jnp.stack(vecs + (none, none)), sel, node_state)
+        bands, edge_w1, edge_w2, node_w1, node_w2, sel, node_state, *vecs)
     node_out, edge_out, node_part, edge_grad, packed, msgs = core(
         bands, parts, edge_count, edge_sender, edge_receiver, edge_state, edge_cot, senders, node_state, node_cot,
         w1, w2, nw1, nw2, vec)

time: 171 us -> 153 us (0.89)
  Pallas kernels: 162 us -> 150 us
  local copies, waits for them, and re-layouts: 5.45 us -> 0 us
    pallas_call x1, Pallas kernels: 87.7 us -> 75.1 us  [core(): pl.pallas_call(functools.partial(core_kernel, nb, R, sub, parts, fast), g...]
    reshape x2 -> x0, local copies, waits for them, and re-layouts: 2.75 us -> none  [the longest x1 1.38 us: core(): sid.reshape(nb, R)]
where the time goes in v3:
time: 153 us; the launch traced here: 152 us
  Pallas kernels  150 us (98%)
    pallas_call x1, Pallas kernels, core(): pl.pallas_call(functools.partial(core_kernel, nb, R, sub, parts, fast), g...  75.1 us
    pallas_call x1, Pallas kernels, reduce_grads(): pl.pallas_call(functools.partial(reduce_kernel, bands), out_shape=[sds((r...  36.6 us
    pallas_call x1, Pallas kernels, gather_weights(): pl.pallas_call(functools.partial(gather_kernel, bands, parts, fast), out_...  35.4 us
    pallas_call x1, Pallas kernels, finish(): pl.pallas_call(functools.partial(finish_kernel, bands, parts), out_shape=...  3.15 us

profile of v3, /device:TPU:0, one launch (start us, length us, event | category | flops | bytes accessed | tf_op | source)
XLA Modules:
  0.0 151.6 jit_solution(8438234036340328102)
XLA Ops:
  1.3 35.4 %gather_weights.1 = (bf16[1536,512]{1,0:T(8,128)(2,1)}, bf16[512,512]{1,0:T(8,128)(2,1)}, bf16[1024,512]{1,0:T(8,128)(2,1)}, bf16[512,512]{1,0:T(8,128)(2,1)}, b...) custom-call(bf16[48,512]{1,0:T(8,128)(2,1)} %w1_ref.1, bf16[16,512]{1,0:T(8,128)(2,1)} %w2_ref.1, ...), custom_call_target="tpu_custom_call" | custom-call | tf_op jit(solution)/shard_map/gather_weights/pallas_call | solution.py:213
  36.7 75.1 %edge_node_core.1 = (bf16[512,512]{1,0:T(8,128)(2,1)}, bf16[8192,512]{1,0:T(8,128)(2,1)}, f32[512,512]{1,0:T(8,128)}, f32[8192,512]{1,0:T(8,128)}, bf16[32,16,25...) custom-call(s32[1]{0:T(128)S(6)} %copy.32.count_ref, s32[64,128]{1,0:T(8,128)} %bitcast.5, s32[64,128]{1,0:T(8,128)} %bitcast.6, ...), custom_call_target="tpu_custom_call" | custom-call | tf_op jit(solution)/shard_map/edge_node_core/pallas_call | solution.py:690
  111.8 36.6 %reduce_grads.1 = (f32[464,128]{1,0:T(8,128)}, bf16[32,16,256]{2,1,0:T(8,128)(2,1)}) custom-call(bf16[2,16,464,128]{3,2,1,0:T(8,128)(2,1)} %get-tuple-element.47.p_ref, bf16[32,16,256]{2,1,0:T(8,128)(2,1)} %get-tuple-element.48.msg_ref), custom_call_target="tpu_custom_call" | custom-call | tf_op jit(solution)/shard_map/reduce_grads/pallas_call | solution.py:348
  148.5 3.1 %finish.1 = (f32[512,512]{1,0:T(8,128)}, f32[48,512]{1,0:T(8,128)}, f32[16,512]{1,0:T(8,128)}, f32[32,512]{1,0:T(8,128)}, f32[16,512]{1,0:T(8,128)}, /*index=5*/...) custom-call(f32[464,128]{1,0:T(8,128)} %get-tuple-element.49.red_ref, ...), custom_call_target="tpu_custom_call" | custom-call | tf_op jit(solution)/shard_map/finish/pallas_call | solution.py:404

commit v4 on v3

--- a/solution.py
+++ b/solution.py
@@ -47,7 +47,7 @@
         return (self.a + k) % self.quads
 
 
-def barrier_all(pos):
+def greet_all(pos):
     sem = pltpu.get_barrier_semaphore()
 
     @pl.loop(1, pos.devices)
@@ -55,116 +55,131 @@
         t = (pos.me + k) % pos.devices
         pl.semaphore_signal(sem, inc=1, device_id=(t // 2, t % 2), device_id_type=MESH)
 
-    pl.semaphore_wait(sem, pos.devices - 1)
-
-
-def gather_kernel(bands, parts, fast, w1_ref, w2_ref, nw1_ref, nw2_ref, sel_ref, node_ref, *refs):
+    return lambda: pl.semaphore_wait(sem, pos.devices - 1)
+
+
+def gather_kernel(bands, parts, w1_ref, w2_ref, nw1_ref, nw2_ref, sel_ref, node_ref, *refs):
     vecs, refs = refs[:6], refs[6:]
-    if fast:
-        outs, (vec_out, snd_out, buf, wide, outg, inc, recv, half, send, a_recv, a_send) = refs[:4], refs[4:]
-    else:
-        (buf, vec_out, snd_out, wide, outg, inc, recv, half, send, a_recv, a_send) = refs
-        outs = None
+    buf, inc, mine, node, wide, outg, recv, half, send_z, send_q, send_h, send_s, a_recv, a_send, own_sem = refs
     pos = Place(bands)
     spots, tail = layout(parts)
-    rows = buf.shape[1]
+    rows = mine.shape[0]
     cut = up16(rows // 2)
-    me, c, a, q = pos.me, pos.c, pos.a, pos.q
-    mats = (w1_ref, w2_ref, nw1_ref, nw2_ref)
-    D = node_ref.shape[1]
+    me, c, a, q, line = pos.me, pos.c, pos.a, pos.q, pos.quads
+    D = node.shape[1]
     slots, peers = sel_ref.shape
-    S = peers * slots
-    for m, p, o in zip(mats, parts, spots):
+    met_all = greet_all(pos)
+    node_copy = pltpu.make_async_copy(node_ref, node, own_sem.at[0])
+    node_copy.start()
+    for m, p, o in zip((w1_ref, w2_ref, nw1_ref, nw2_ref), parts, spots):
         for j in range(4):
-            buf[me, o + j * up16(p):o + j * up16(p) + p, :] = m[:, 128 * j:128 * j + 128]
+            mine[o + j * up16(p):o + j * up16(p) + p, :] = m[:, 128 * j:128 * j + 128]
     width = vecs[0].shape[0]
     group = 128 // width
     lanes = lax.broadcasted_iota(jnp.int32, (1, 128), 1)
-    for k in range(16):
-        if k < 6:
-            val = jnp.concatenate([vecs[k][...].astype(F32).reshape(1, width)] * group, axis=1)
-            wide[k:k + 1, :] = jnp.where(lanes // width == me % group, val, 0.0)
-        else:
-            wide[k:k + 1, :] = jnp.zeros((1, 128), F32)
-    buf[me, tail:tail + 16, :] = wide[...].astype(BF)
-    barrier_all(pos)
-    count = [0]
-
-    def push(src, part, sem, target):
-        ref = buf.at[src] if part is None else buf.at[src, part]
-        cp = pltpu.make_async_remote_copy(src_ref=ref, dst_ref=ref, send_sem=send.at[count[0]], recv_sem=sem,
-                                          device_id=target, device_id_type=MESH)
-        count[0] += 1
-        cp.start()
-        return cp
-
-    started = []
-    A_PART, B_PART = pl.ds(0, cut), pl.ds(cut, rows - cut)
-
-    def wait(src, part, sem):
-        ref = buf.at[src] if part is None else buf.at[src, part]
-        pltpu.make_async_remote_copy(src_ref=ref, dst_ref=ref, send_sem=send.at[0], recv_sem=sem,
-                                     device_id=pos.dev(a, q, 1 - c), device_id_type=MESH).wait_recv()
-
-    def unpack(src):
-        if outs is None:
-            return
-        for o_ref, p, o in zip(outs, parts, spots):
-            for j in range(4):
-                o_ref[pl.ds(pl.multiple_of(src * p, 16), p), 128 * j:128 * j + 128] = \
-                    buf[src, o + j * p:o + j * p + p, :]
-
-    for k in range(1, pos.quads):
-        started.append(push(me, None, recv.at[me], pos.dev(pos.other_a(k), q, c)))
-
-    def spread(src):
-        started.append(push(src, None, recv.at[src], pos.dev(a, pos.qx, c)))
-        started.append(push(src, None, recv.at[src], pos.dev(a, pos.qy, c)))
-
-    def sibling(src):
-        started.append(push(src, None, recv.at[src], pos.dev(a, q, 1 - c)))
-
-    spread(me)
-    sibling(me)
-    hot = slot_onehot(sel_ref[...], node_ref.shape[0])
-    picked = jnp.dot(hot, node_ref[...], preferred_element_type=F32)
+    wide[...] = jnp.zeros_like(wide)
+    for k in range(6):
+        val = jnp.concatenate([vecs[k][...].astype(F32).reshape(1, width)] * group, axis=1)
+        wide[k:k + 1, :] = jnp.where(lanes // width == me % group, val, 0.0)
+    mine[tail:tail + 16, :] = wide[...].astype(BF)
+    own_copy = pltpu.make_async_copy(mine, buf.at[me], own_sem.at[1])
+    own_copy.start()
+    hot = slot_onehot(sel_ref[...], node.shape[0])
+    node_copy.wait()
+    picked = jnp.dot(hot, node[...], preferred_element_type=F32)
     outg[:, 0:slots, :] = picked[:, 0:D // 2].reshape(peers, slots, D // 2).astype(BF)
     outg[:, slots:, :] = picked[:, D // 2:].reshape(peers, slots, D // 2).astype(BF)
+    msg_copy = pltpu.make_async_copy(outg.at[me], inc.at[me], own_sem.at[2])
+    msg_copy.start()
+    met_all()
+
+    WHOLE = pl.ds(0, rows)
+    FIRST, LAST = pl.ds(0, cut), pl.ds(cut, rows - cut)
+
+    def push(ak, qk, part, sem_send, sem_recv, target, own=False):
+        src = pos.idx(ak, qk, c)
+        return pltpu.make_async_remote_copy(
+            src_ref=mine.at[part] if own else buf.at[src, part], dst_ref=buf.at[src, part],
+            send_sem=sem_send, recv_sem=sem_recv, device_id=target, device_id_type=MESH)
+
+    def up(ak, own=False):
+        return push(ak, q, WHOLE, send_z.at[0, ak], recv.at[pos.idx(ak, q, c)], pos.dev(a + 1, q, c), own)
+
+    def down(ak, own=False):
+        return push(ak, q, WHOLE, send_z.at[1, ak], recv.at[pos.idx(ak, q, c)], pos.dev(a - 1, q, c), own)
+
+    def to_x(ak, own=False):
+        return push(ak, q, WHOLE, send_q.at[0, ak], recv.at[pos.idx(ak, q, c)], pos.dev(a, pos.qx, c), own)
+
+    def to_y(ak, own=False):
+        return push(ak, q, WHOLE, send_q.at[1, ak], recv.at[pos.idx(ak, q, c)], pos.dev(a, pos.qy, c), own)
+
+    def x_to_y(ak):
+        return push(ak, pos.qx, FIRST, send_h.at[0, ak], half.at[0, ak], pos.dev(a, pos.qy, c))
+
+    def y_to_x(ak):
+        return push(ak, pos.qy, LAST, send_h.at[1, ak], half.at[1, ak], pos.dev(a, pos.qx, c))
+
+    def sibling(ak, qk, own=False):
+        return push(ak, qk, WHOLE, send_s.at[ak * LINE + qk], recv.at[pos.idx(ak, qk, c)], pos.dev(a, q, 1 - c), own)
+
+    def arrive(ak, qk, ck=None):
+        src = pos.idx(ak, qk, c if ck is None else ck)
+        pltpu.make_async_remote_copy(src_ref=buf.at[src], dst_ref=buf.at[src], send_sem=send_s.at[0],
+                                     recv_sem=recv.at[src], device_id=pos.dev(a, q, 1 - c),
+                                     device_id_type=MESH).wait_recv()
 
     def exchange(t):
         return pltpu.make_async_remote_copy(src_ref=outg.at[t], dst_ref=inc.at[me], send_sem=a_send.at[t],
                                             recv_sem=a_recv.at[me], device_id=(t // 2, t % 2), device_id_type=MESH)
 
+    pl.when(a + 1 < line)(lambda: up(a, True).start())
+    pl.when(a > 0)(lambda: down(a, True).start())
+    to_x(a, True).start()
+    to_y(a, True).start()
+    sibling(a, q, True).start()
+
+    def along(ak, below):
+        arrive(ak, q)
+        if below:
+            pl.when(a + 1 < line)(lambda: up(ak).start())
+        else:
+            pl.when(a > 0)(lambda: down(ak).start())
+        to_x(ak).start()
+        to_y(ak).start()
+        sibling(ak, q).start()
+
+    def square(ak):
+        arrive(ak, pos.qx)
+        x_to_y(ak).start()
+        sibling(ak, pos.qx).start()
+        arrive(ak, pos.qy)
+        y_to_x(ak).start()
+        sibling(ak, pos.qy).start()
+
+    def both(k, what):
+        pl.when(a - k >= 0)(lambda: what(a - k, True))
+        pl.when(a + k < line)(lambda: what(a + k, False))
+
+    for k in range(1, line):
+        both(k, along)
+        if k == 1:
+            square(a)
+        else:
+            both(k - 1, lambda ak, below: square(ak))
+    both(line - 1, lambda ak, below: square(ak))
+
     @pl.loop(1, pos.devices)
     def _(k):
         exchange((me + k) % pos.devices).start()
 
-    inc[me] = outg[me]
-    unpack(me)
-    line = [pos.idx(pos.other_a(k), q, c) for k in range(1, pos.quads)]
-    for src in line:
-        wait(src, None, recv.at[src])
-        spread(src)
-        sibling(src)
-        unpack(src)
-    for k in range(pos.quads):
+    for k in range(line):
         ak = pos.other_a(k)
-        sx, sy = pos.idx(ak, pos.qx, c), pos.idx(ak, pos.qy, c)
-        wait(sx, None, recv.at[sx])
-        started.append(push(sx, A_PART, half.at[0, ak], pos.dev(a, pos.qy, c)))
-        sibling(sx)
-        unpack(sx)
-        wait(sy, None, recv.at[sy])
-        started.append(push(sy, B_PART, half.at[1, ak], pos.dev(a, pos.qx, c)))
-        sibling(sy)
-        unpack(sy)
-    for k in range(pos.quads):
-        ak = pos.other_a(k)
-        sd = pos.idx(ak, pos.qd, c)
-        wait(sd, A_PART, half.at[0, ak])
-        wait(sd, B_PART, half.at[1, ak])
-        sibling(sd)
-        unpack(sd)
+        for part, at in ((FIRST, 0), (LAST, 1)):
+            ref = buf.at[pos.idx(ak, pos.qd, c), part]
+            pltpu.make_async_remote_copy(src_ref=ref, dst_ref=ref, send_sem=send_s.at[0], recv_sem=half.at[at, ak],
+                                         device_id=pos.dev(a, q, 1 - c), device_id_type=MESH).wait_recv()
+        sibling(ak, pos.qd).start()
 
     @pl.loop(1, pos.devices)
     def _(k):
@@ -172,59 +187,39 @@
         pltpu.make_async_remote_copy(src_ref=outg.at[t], dst_ref=inc.at[t], send_sem=a_send.at[t],
                                      recv_sem=a_recv.at[t], device_id=(t // 2, t % 2), device_id_type=MESH).wait()
 
-    snd_out[:, 0:D // 2] = inc[:, 0:slots, :].astype(F32).reshape(S, D // 2).astype(BF)
-    snd_out[:, D // 2:] = inc[:, slots:, :].astype(F32).reshape(S, D // 2).astype(BF)
-    for k in range(pos.quads):
+    own_copy.wait()
+    msg_copy.wait()
+    for k in range(line):
         ak = pos.other_a(k)
-        for qq in (q, pos.qx, pos.qy, pos.qd):
-            src = pos.idx(ak, qq, 1 - c)
-            wait(src, None, recv.at[src])
-            unpack(src)
-    for g in range(D // 128):
-        v = buf[g * group, tail:tail + 16, :].astype(F32)
-        for s in range(1, group):
-            v = v + buf[g * group + s, tail:tail + 16, :].astype(F32)
-        vec_out[:, 128 * g:128 * g + 128] = v.astype(BF)
-    for cp in started:
-        cp.wait_send()
+        pl.when((a + 1 < line) & (ak <= a))(lambda: up(ak).wait_send())
+        pl.when((a > 0) & (ak >= a))(lambda: down(ak).wait_send())
+        for cp in (to_x(ak), to_y(ak), x_to_y(ak), y_to_x(ak)):
+            cp.wait_send()
+        for qk in (q, pos.qx, pos.qy, pos.qd):
+            sibling(ak, qk).wait_send()
+            arrive(ak, qk, 1 - c)
 
 
 def gather_weights(bands, w1, w2, nw1, nw2, sel, node, *vecs):
     parts = tuple(m.shape[0] for m in (w1, w2, nw1, nw2))
-    fast = all(p % 16 == 0 for p in parts)
-    _, tail = layout(parts)
-    rows = tail + 16
-    n = bands * 2
-    quads = bands // LINE
+    rows = layout(parts)[1] + 16
+    n, line = bands * 2, bands // LINE
     D = node.shape[1]
     slots, peers = sel.shape
-    S = peers * slots
-    V = pl.BlockSpec(memory_space=pltpu.VMEM)
-    sds = jax.ShapeDtypeStruct
-    shards = sds((n, rows, 128), BF)
-    full = [sds((n * p, D), BF) for p in parts]
-    outs = (full if fast else [shards]) + [sds((16, D), BF), sds((S, D), BF)]
-    sends = (quads - 1) + 2 * quads + 2 * quads + 4 * quads
-    scratch = ([pltpu.VMEM(shards.shape, BF)] if fast else []) + [
-        pltpu.VMEM((16, 128), F32),
-        pltpu.VMEM((peers, 2 * slots, D // 2), BF), pltpu.VMEM((peers, 2 * slots, D // 2), BF),
-        pltpu.SemaphoreType.DMA((n,)), pltpu.SemaphoreType.DMA((2, quads)), pltpu.SemaphoreType.DMA((sends,)),
-        pltpu.SemaphoreType.DMA((n,)), pltpu.SemaphoreType.DMA((n,))]
-    res = pl.pallas_call(
-        functools.partial(gather_kernel, bands, parts, fast),
-        out_shape=outs, in_specs=[V] * 12, out_specs=[V] * len(outs), scratch_shapes=scratch,
-        compiler_params=pltpu.CompilerParams(collective_id=0, has_side_effects=True, vmem_limit_bytes=60 * 2**20),
+    V, H = pl.BlockSpec(memory_space=pltpu.VMEM), pl.BlockSpec(memory_space=pl.ANY)
+    sds, sem, vm = jax.ShapeDtypeStruct, pltpu.SemaphoreType.DMA, pltpu.VMEM
+    msgs = (peers, 2 * slots, D // 2)
+    return pl.pallas_call(
+        functools.partial(gather_kernel, bands, parts),
+        out_shape=[sds((n, rows, 128), BF), sds(msgs, BF)],
+        in_specs=[V] * 5 + [H] + [V] * 6, out_specs=[H, H],
+        scratch_shapes=[
+            vm((rows, 128), BF), vm(node.shape, BF), vm((16, 128), F32), vm(msgs, BF),
+            sem((n,)), sem((2, line)), sem((2, line)), sem((2, line)), sem((2, line)), sem((bands,)),
+            sem((n,)), sem((n,)), sem((3,))],
+        compiler_params=pltpu.CompilerParams(collective_id=0, has_side_effects=True, vmem_limit_bytes=63 * 2**20),
         name="gather_weights",
     )(w1, w2, nw1, nw2, sel, node, *vecs)
-    if fast:
-        return res
-    got, vec, snd = res
-    spots, _ = layout(parts)
-    mats = []
-    for p, o in zip(parts, spots):
-        cols = [got[:, o + j * up16(p):o + j * up16(p) + p, :].reshape(n * p, 128) for j in range(4)]
-        mats.append(jnp.concatenate(cols, axis=1))
-    return (*mats, vec, snd)
 
 
 def reduce_kernel(bands, p_ref, msg_ref, red_ref, arr_ref, own, sib, xa, yb, ya, xb, zin,
@@ -255,7 +250,7 @@
         cp = pltpu.make_async_copy(p_ref.at[c, sq], own.at[sq], own_sem.at[ak])
         cp.start()
         mine.append(cp)
-    barrier_all(pos)
+    greet_all(pos)()
     for ak, sq in zip(order, square):
         push(p_ref.at[1 - c, sq], sib.at[sq], sib_recv.at[ak], pos.dev(a, q, 1 - c))
 
@@ -356,7 +351,7 @@
             pltpu.VMEM((quads, rows, 128), BF),
             sem((quads,)), sem((quads,)), sem((quads, 2)), sem((quads, 2)), sem((quads,)), sem((quads,)), sem((quads,)),
             sem((8 * quads,)), sem((n,)), sem((n,))],
-        compiler_params=pltpu.CompilerParams(collective_id=1, has_side_effects=True, vmem_limit_bytes=60 * 2**20),
+        compiler_params=pltpu.CompilerParams(collective_id=1, has_side_effects=True, vmem_limit_bytes=63 * 2**20),
         name="reduce_grads",
     )(packed, msgs)
 
@@ -404,7 +399,7 @@
     return pl.pallas_call(
         functools.partial(finish_kernel, bands, parts),
         out_shape=outs, in_specs=[V] * 4, out_specs=[V] * len(outs),
-        compiler_params=pltpu.CompilerParams(vmem_limit_bytes=60 * 2**20),
+        compiler_params=pltpu.CompilerParams(vmem_limit_bytes=63 * 2**20),
         name="finish",
     )(red, arrived, sel, part)
 
@@ -443,18 +438,19 @@
     return jnp.sum(v.reshape(v.shape[0] // 8, 8, v.shape[1]), axis=0)
 
 
-def core_kernel(nb, R, sub, parts, fast, count_ref, sid_ref, rid_ref, e_ref, cot_ref, snd_ref, node_ref, ncot_ref,
-                w1_ref, w2_ref, nw1_ref, nw2_ref, vec_ref,
-                nout_ref, eout_ref, ngrad_ref, egrad_ref, msg_ref, *refs):
+def core_kernel(nb, R, sub, parts, fast, count_ref, sid_ref, rid_ref, e_ref, cot_ref, node_ref, ncot_ref, *refs):
+    (got_ref, inc_ref), refs = (refs[:2], refs[2:]) if fast else ((None, None), refs)
+    weights, refs = ((), refs) if fast else (refs[:6], refs[6:])
+    nout_ref, eout_ref, ngrad_ref, egrad_ref, msg_ref, *refs = refs
     outs, refs = (refs[:1], refs[1:]) if fast else (refs[:5], refs[5:])
-    wcat, w2h, hid_s, slope_s, nrm_s, scale_s, gath, dg, gacc, g2acc, gain_acc, shift_acc, gvec, msg_s, dpre_s, w1t = refs
+    weights, refs = (refs[:6], refs[6:]) if fast else (weights, refs)
+    w1_ref, w2_ref, nw1_ref, nw2_ref, vec_ref, snd_ref = weights
+    wcat, w2h, hid_s, slope_s, nrm_s, scale_s, gath, dg, gacc, g2acc, gain_acc, shift_acc, gvec, msg_s, dpre_s, w1t, sem = refs
     i = pl.program_id(0)
     D = e_ref.shape[1]
     S = snd_ref.shape[0]
     N = node_ref.shape[0]
     count = count_ref[0]
-    gain = vec_ref[1:2, :].astype(F32)
-    shift = vec_ref[2:3, :].astype(F32)
     spots, tail = layout(parts)
     n = 3 * D // parts[0]
 
@@ -470,8 +466,32 @@
                 at = o + j * p + a - d * p
                 outs[0][d % 2, d // 2, at:at + b - a, :] = value[a - lo:b - lo, 128 * j:128 * j + 128].astype(BF)
 
+    def unpack():
+        stage = outs[0]
+        cp = pltpu.make_async_copy(got_ref, stage, sem)
+        cp.start()
+        cp.wait()
+
+        @pl.loop(0, n)
+        def _(d):
+            for w_ref, p, o in zip((w1_ref, w2_ref, nw1_ref, nw2_ref), parts, spots):
+                for j in range(D // 128):
+                    w_ref[pl.ds(pl.multiple_of(d * p, p), p), 128 * j:128 * j + 128] = \
+                        stage[d // (n // 2), d % (n // 2), o + j * p:o + j * p + p, :]
+
+        group = n // (D // 128)
+        for g in range(D // 128):
+            tiles = [stage[d // (n // 2), d % (n // 2), tail:tail + 16, :].astype(F32)
+                     for d in range(g * group, (g + 1) * group)]
+            vec_ref[:, 128 * g:128 * g + 128] = functools.reduce(jnp.add, tiles).astype(BF)
+        slots = inc_ref.shape[1] // 2
+        snd_ref[:, 0:D // 2] = inc_ref[:, 0:slots, :].astype(F32).reshape(S, D // 2).astype(BF)
+        snd_ref[:, D // 2:] = inc_ref[:, slots:, :].astype(F32).reshape(S, D // 2).astype(BF)
+
     @pl.when(i == 0)
     def _():
+        if fast:
+            unpack()
         b1 = vec_ref[0:1, :].astype(F32)
         wcat[0:D, :] = w1_ref[0:D, :] * 0.5
         wcat[D:D + S, :] = (dot(snd_ref[...], w1_ref[D:2 * D, :]) * 0.5).astype(BF)
@@ -485,6 +505,8 @@
         shift_acc[...] = jnp.zeros_like(shift_acc)
         scale_s[...] = jnp.zeros_like(scale_s)
 
+    gain = vec_ref[1:2, :].astype(F32)
+    shift = vec_ref[2:3, :].astype(F32)
     blk = lax.rem(i, nb)
     live_blk = blk * R < count
     subs = R // sub
@@ -518,7 +540,7 @@
             v = h[r]
             a = 1.0 + jnp.tanh(v)
             hid = v * a
-            slope_s[rows[r], :] = (a * (1.0 + 2.0 * v - hid)).astype(BF)
+            slope_s[rows[r], :] = (a + hid * (2.0 - a)).astype(BF)
             hid_s[rows[r], :] = hid.astype(BF)
 
         def b1(r):
@@ -669,40 +691,55 @@
                     [gvec[:, 128 * g:128 * g + 128]] * 2, axis=0).astype(BF)
 
 
-def core(bands, parts, count, sid, rid, e, cot, snd, node, ncot, w1, w2, nw1, nw2, vec, sub=128):
+def core(bands, parts, count, sid, rid, e, cot, node, ncot, got, inc, sub=128):
     E, D = e.shape
-    R = 1024 if snd.shape[0] <= 256 else 512
+    S, N = inc.shape[0] * inc.shape[1] // 2, node.shape[0]
+    R = 1024 if S <= 256 else 512
     nb = E // R
-    S, N = snd.shape[0], node.shape[0]
-    V = pl.BlockSpec(memory_space=pltpu.VMEM)
+    V, H = pl.BlockSpec(memory_space=pltpu.VMEM), pl.BlockSpec(memory_space=pl.ANY)
     fb = pl.BlockSpec((R, D), lambda i: (jnp.minimum(i, nb - 1), 0))
     bb = pl.BlockSpec((R, D), lambda i: (jnp.maximum(i - nb, 0), 0))
     both = pl.BlockSpec((R, D), lambda i: (lax.rem(i, nb), 0))
-    sds = jax.ShapeDtypeStruct
-    slots = S // (2 * bands)
+    sds, vm = jax.ShapeDtypeStruct, pltpu.VMEM
     fast = all(p % 16 == 0 for p in parts)
     rows = layout(parts)[1] + 16
+    if fast:
+        weights, specs = (got.reshape(2, bands, rows, 128), inc), [H, V]
+    else:
+        weights, specs = unpack_weights(bands, parts, got, inc), [V] * 6
     grads = [(3 * D, D), (D, D), (2 * D, D), (D, D), (8, D)]
-    outs = [sds((N, D), BF), sds((E, D), BF), sds((N, D), F32), sds((E, D), F32),
-            sds((2 * bands, 2 * slots, D // 2), BF)]
+    outs = [sds((N, D), BF), sds((E, D), BF), sds((N, D), F32), sds((E, D), F32), sds(inc.shape, BF)]
     outs += [sds((2, bands, rows, 128), BF)] if fast else [sds(g, F32) for g in grads]
-    vm = pltpu.VMEM
     *res, packed = res = pl.pallas_call(
         functools.partial(core_kernel, nb, R, sub, parts, fast),
         grid=(2 * nb,),
-        in_specs=[pl.BlockSpec(memory_space=pltpu.SMEM), V, V, both, bb, V, V, V, V, V, V, V, V],
+        in_specs=[pl.BlockSpec(memory_space=pltpu.SMEM), V, V, both, bb, V, V] + specs,
         out_specs=[V, fb, V, bb] + [V] * (len(outs) - 4),
         out_shape=outs,
-        scratch_shapes=[
+        scratch_shapes=([vm(g, BF) for g in grads[:4]] + [vm((16, D), BF), vm((S, D), BF)] if fast else []) + [
             vm((D + S + N, D), BF), vm((D, D), BF), vm((E, D), BF), vm((E, D), BF), vm((E, D), BF),
             vm((sub, 128), F32), vm((N, D), F32), vm((N, D), BF), vm((D + S + N, D), F32), vm((D, D), F32),
-            vm((8, D), F32), vm((8, D), F32), vm((8, D), F32), vm((R, D), BF), vm((R, D), BF), vm((D, D), BF)],
+            vm((8, D), F32), vm((8, D), F32), vm((8, D), F32), vm((R, D), BF), vm((R, D), BF), vm((D, D), BF),
+            pltpu.SemaphoreType.DMA],
         compiler_params=pltpu.CompilerParams(vmem_limit_bytes=63 * 2**20, dimension_semantics=("arbitrary",)),
         name="edge_node_core",
-    )(count, sid.reshape(E // sub, sub), rid.reshape(E // sub, sub), e, cot, snd, node, ncot, w1, w2, nw1, nw2, vec)
+    )(count, sid.reshape(E // sub, sub), rid.reshape(E // sub, sub), e, cot, node, ncot, *weights)
     if not fast:
         packed = pack_grads(bands, parts, res[5:])
     return (*res[:4], packed, res[4])
+
+
+def unpack_weights(bands, parts, got, inc):
+    spots, tail = layout(parts)
+    n, slots, D = 2 * bands, inc.shape[1] // 2, 2 * inc.shape[2]
+    mats = []
+    for p, o in zip(parts, spots):
+        cols = [got[:, o + j * up16(p):o + j * up16(p) + p, :].reshape(n * p, 128) for j in range(D // 128)]
+        mats.append(jnp.concatenate(cols, axis=1))
+    slabs = got[:, tail:tail + 16, :].reshape(D // 128, -1, 16, 128).sum(axis=1)
+    vec = slabs.transpose(1, 0, 2).reshape(16, D)
+    snd = jnp.concatenate([inc[:, :slots].reshape(n * slots, D // 2), inc[:, slots:].reshape(n * slots, D // 2)], axis=1)
+    return (*mats, vec, snd)
 
 
 def pack_grads(bands, parts, grads):
@@ -724,11 +761,9 @@
     width = edge_b1.shape[0]
     vecs = (edge_b1, edge_gain, edge_shift, node_b1, node_gain, node_shift)
     sel = send_rows[0].T
-    w1, w2, nw1, nw2, vec, senders = gather_weights(
-        bands, edge_w1, edge_w2, node_w1, node_w2, sel, node_state, *vecs)
+    got, inc = gather_weights(bands, edge_w1, edge_w2, node_w1, node_w2, sel, node_state, *vecs)
     node_out, edge_out, node_part, edge_grad, packed, msgs = core(
-        bands, parts, edge_count, edge_sender, edge_receiver, edge_state, edge_cot, senders, node_state, node_cot,
-        w1, w2, nw1, nw2, vec)
+        bands, parts, edge_count, edge_sender, edge_receiver, edge_state, edge_cot, node_state, node_cot, got, inc)
     red, arrived = reduce_grads(bands, packed, msgs)
     node_grad, gw1, gw2, gnw1, gnw2, *gv = finish(bands, parts, width, red, arrived, sel, node_part)
     return (node_out, edge_out, node_grad, edge_grad, gw1, gv[0], gw2, gv[1], gv[2], gnw1, gv[3], gnw2, gv[4], gv[5])

time: 153 us -> 146 us (0.954)
  Pallas kernels: 150 us -> 145 us
    pallas_call x1, Pallas kernels: 75.1 us -> 68.9 us  [core(): pl.pallas_call(functools.partial(core_kernel, nb, R, sub, parts, fast), g...]
    pallas_call x1, Pallas kernels: 36.6 us -> 40.5 us  [reduce_grads(): pl.pallas_call(functools.partial(reduce_kernel, bands), out_shape=[sds((r...]
    pallas_call x1, Pallas kernels: 35.4 us -> 32.2 us  [gather_weights(): pl.pallas_call(functools.partial(gather_kernel, bands, parts), out_shape=...]
where the time goes in v4:
time: 146 us
  Pallas kernels  145 us (99%)
    pallas_call x1, Pallas kernels, core(): pl.pallas_call(functools.partial(core_kernel, nb, R, sub, parts, fast), g...  68.9 us
    pallas_call x1, Pallas kernels, reduce_grads(): pl.pallas_call(functools.partial(reduce_kernel, bands), out_shape=[sds((r...  40.5 us
    pallas_call x1, Pallas kernels, gather_weights(): pl.pallas_call(functools.partial(gather_kernel, bands, parts), out_shape=...  32.2 us
    pallas_call x1, Pallas kernels, finish(): pl.pallas_call(functools.partial(finish_kernel, bands, parts), out_shape=...  3.14 us

profile of v4, /device:TPU:0, one launch (start us, length us, event | category | flops | bytes accessed | tf_op | source)
XLA Modules:
  0.0 146.0 jit_solution(4972680829270752849)
XLA Ops:
  1.3 32.2 %gather_weights.1 = (bf16[32,464,128]{2,1,0:T(8,128)(2,1)}, bf16[32,16,256]{2,1,0:T(8,128)(2,1)}) custom-call(bf16[48,512]{1,0:T(8,128)(2,1)} %w1_ref.1, bf16[16,512]{1,0:T(8,128)(2,1)} %w2_ref.1, bf16[32,512]{1,0:T(8,128)(2,1)} %nw1_ref.1, bf16[16,512]{1,0:T(8,128)(2,1)} %nw2_ref.1, s32[8,32]{1,0:T(8,128)} %bitcast.9, bf16[512,512]{1,0:T(8,128)(2,1)} %node_ref.3, ...), custom_call_target="tpu_custom_call" | custom-call | tf_op jit(solution)/shard_map/gather_weights/pallas_call | solution.py:212
  33.5 68.9 %edge_node_core.1 = (bf16[512,512]{1,0:T(8,128)(2,1)}, bf16[8192,512]{1,0:T(8,128)(2,1)}, f32[512,512]{1,0:T(8,128)}, f32[8192,512]{1,0:T(8,128)}, bf16[32,16,25...) custom-call(s32[1]{0:T(128)S(6)} %copy.32.count_ref, s32[64,128]{1,0:T(8,128)} %bitcast.7, s32[64,128]{1,0:T(8,128)} %bitcast.8, ...), custom_call_target="tpu_custom_call" | custom-call | tf_op jit(solution)/shard_map/edge_node_core/pallas_call | solution.py:713
  102.4 40.5 %reduce_grads.1 = (f32[464,128]{1,0:T(8,128)}, bf16[32,16,256]{2,1,0:T(8,128)(2,1)}) custom-call(bf16[2,16,464,128]{3,2,1,0:T(8,128)(2,1)} %get-tuple-element.39.p_ref, bf16[32,16,256]{2,1,0:T(8,128)(2,1)} %get-tuple-element.40.msg_ref), custom_call_target="tpu_custom_call" | custom-call | tf_op jit(solution)/shard_map/reduce_grads/pallas_call | solution.py:343
  142.9 3.1 %finish.1 = (f32[512,512]{1,0:T(8,128)}, f32[48,512]{1,0:T(8,128)}, f32[16,512]{1,0:T(8,128)}, f32[32,512]{1,0:T(8,128)}, f32[16,512]{1,0:T(8,128)}, /*index=5*/...) custom-call(f32[464,128]{1,0:T(8,128)} %get-tuple-element.41.red_ref, ...), custom_call_target="tpu_custom_call" | custom-call | tf_op jit(solution)/shard_map/finish/pallas_call | solution.py:399

commit v5 on v4

--- a/solution.py
+++ b/solution.py
@@ -58,19 +58,26 @@
     return lambda: pl.semaphore_wait(sem, pos.devices - 1)
 
 
-def gather_kernel(bands, parts, w1_ref, w2_ref, nw1_ref, nw2_ref, sel_ref, node_ref, *refs):
-    vecs, refs = refs[:6], refs[6:]
-    buf, inc, mine, node, wide, outg, recv, half, send_z, send_q, send_h, send_s, a_recv, a_send, own_sem = refs
+def gather_kernel(bands, parts, *refs):
+    inputs, refs = refs[:12], refs[12:]
+    buf, inc, mine, node, wide, outg, recv, half, send_z, send_q, send_h, send_s, a_recv, a_send, own_sem, in_sem, *held = refs
     pos = Place(bands)
     spots, tail = layout(parts)
     rows = mine.shape[0]
     cut = up16(rows // 2)
     me, c, a, q, line = pos.me, pos.c, pos.a, pos.q, pos.quads
+    w1_ref, w2_ref, nw1_ref, nw2_ref, sel_ref = held[:5]
+    vecs = held[5:]
     D = node.shape[1]
     slots, peers = sel_ref.shape
     met_all = greet_all(pos)
-    node_copy = pltpu.make_async_copy(node_ref, node, own_sem.at[0])
+    fetched = [pltpu.make_async_copy(h, v, in_sem.at[k]) for k, (h, v) in enumerate(zip(inputs, held))]
+    node_copy = pltpu.make_async_copy(inputs[11], node, own_sem.at[0])
+    for cp in fetched:
+        cp.start()
     node_copy.start()
+    for cp in fetched:
+        cp.wait()
     for m, p, o in zip((w1_ref, w2_ref, nw1_ref, nw2_ref), parts, spots):
         for j in range(4):
             mine[o + j * up16(p):o + j * up16(p) + p, :] = m[:, 128 * j:128 * j + 128]
@@ -84,6 +91,54 @@
     mine[tail:tail + 16, :] = wide[...].astype(BF)
     own_copy = pltpu.make_async_copy(mine, buf.at[me], own_sem.at[1])
     own_copy.start()
+    met_all()
+
+    WHOLE = pl.ds(0, rows)
+    FIRST, LAST = pl.ds(0, cut), pl.ds(cut, rows - cut)
+
+    def push(ak, qk, part, sem_send, sem_recv, target, own=False):
+        src = pos.idx(ak, qk, c)
+        return pltpu.make_async_remote_copy(
+            src_ref=mine.at[part] if own else buf.at[src, part], dst_ref=buf.at[src, part],
+            send_sem=sem_send, recv_sem=sem_recv, device_id=target, device_id_type=MESH)
+
+    def up(ak, own=False):
+        return push(ak, q, WHOLE, send_z.at[0, ak], recv.at[pos.idx(ak, q, c)], pos.dev(a + 1, q, c), own)
+
+    def down(ak, own=False):
+        return push(ak, q, WHOLE, send_z.at[1, ak], recv.at[pos.idx(ak, q, c)], pos.dev(a - 1, q, c), own)
+
+    def to_x(ak, own=False):
+        return push(ak, q, WHOLE, send_q.at[0, ak], recv.at[pos.idx(ak, q, c)], pos.dev(a, pos.qx, c), own)
+
+    def to_y(ak, own=False):
+        return push(ak, q, WHOLE, send_q.at[1, ak], recv.at[pos.idx(ak, q, c)], pos.dev(a, pos.qy, c), own)
+
+    def x_to_y(ak):
+        return push(ak, pos.qx, FIRST, send_h.at[0, ak], half.at[0, ak], pos.dev(a, pos.qy, c))
+
+    def y_to_x(ak):
+        return push(ak, pos.qy, LAST, send_h.at[1, ak], half.at[1, ak], pos.dev(a, pos.qx, c))
+
+    def sibling(ak, qk, own=False):
+        return push(ak, qk, WHOLE, send_s.at[ak * LINE + qk], recv.at[pos.idx(ak, qk, c)], pos.dev(a, q, 1 - c), own)
+
+    def arrive(ak, qk, ck=None):
+        src = pos.idx(ak, qk, c if ck is None else ck)
+        pltpu.make_async_remote_copy(src_ref=buf.at[src], dst_ref=buf.at[src], send_sem=send_s.at[0],
+                                     recv_sem=recv.at[src], device_id=pos.dev(a, q, 1 - c),
+                                     device_id_type=MESH).wait_recv()
+
+    def exchange(t):
+        return pltpu.make_async_remote_copy(src_ref=outg.at[t], dst_ref=inc.at[me], send_sem=a_send.at[t],
+                                            recv_sem=a_recv.at[me], device_id=(t // 2, t % 2), device_id_type=MESH)
+
+    pl.when(a + 1 < line)(lambda: up(a, True).start())
+    pl.when(a > 0)(lambda: down(a, True).start())
+    to_x(a, True).start()
+    to_y(a, True).start()
+    sibling(a, q, True).start()
+
     hot = slot_onehot(sel_ref[...], node.shape[0])
     node_copy.wait()
     picked = jnp.dot(hot, node[...], preferred_element_type=F32)
@@ -91,53 +146,6 @@
     outg[:, slots:, :] = picked[:, D // 2:].reshape(peers, slots, D // 2).astype(BF)
     msg_copy = pltpu.make_async_copy(outg.at[me], inc.at[me], own_sem.at[2])
     msg_copy.start()
-    met_all()
-
-    WHOLE = pl.ds(0, rows)
-    FIRST, LAST = pl.ds(0, cut), pl.ds(cut, rows - cut)
-
-    def push(ak, qk, part, sem_send, sem_recv, target, own=False):
-        src = pos.idx(ak, qk, c)
-        return pltpu.make_async_remote_copy(
-            src_ref=mine.at[part] if own else buf.at[src, part], dst_ref=buf.at[src, part],
-            send_sem=sem_send, recv_sem=sem_recv, device_id=target, device_id_type=MESH)
-
-    def up(ak, own=False):
-        return push(ak, q, WHOLE, send_z.at[0, ak], recv.at[pos.idx(ak, q, c)], pos.dev(a + 1, q, c), own)
-
-    def down(ak, own=False):
-        return push(ak, q, WHOLE, send_z.at[1, ak], recv.at[pos.idx(ak, q, c)], pos.dev(a - 1, q, c), own)
-
-    def to_x(ak, own=False):
-        return push(ak, q, WHOLE, send_q.at[0, ak], recv.at[pos.idx(ak, q, c)], pos.dev(a, pos.qx, c), own)
-
-    def to_y(ak, own=False):
-        return push(ak, q, WHOLE, send_q.at[1, ak], recv.at[pos.idx(ak, q, c)], pos.dev(a, pos.qy, c), own)
-
-    def x_to_y(ak):
-        return push(ak, pos.qx, FIRST, send_h.at[0, ak], half.at[0, ak], pos.dev(a, pos.qy, c))
-
-    def y_to_x(ak):
-        return push(ak, pos.qy, LAST, send_h.at[1, ak], half.at[1, ak], pos.dev(a, pos.qx, c))
-
-    def sibling(ak, qk, own=False):
-        return push(ak, qk, WHOLE, send_s.at[ak * LINE + qk], recv.at[pos.idx(ak, qk, c)], pos.dev(a, q, 1 - c), own)
-
-    def arrive(ak, qk, ck=None):
-        src = pos.idx(ak, qk, c if ck is None else ck)
-        pltpu.make_async_remote_copy(src_ref=buf.at[src], dst_ref=buf.at[src], send_sem=send_s.at[0],
-                                     recv_sem=recv.at[src], device_id=pos.dev(a, q, 1 - c),
-                                     device_id_type=MESH).wait_recv()
-
-    def exchange(t):
-        return pltpu.make_async_remote_copy(src_ref=outg.at[t], dst_ref=inc.at[me], send_sem=a_send.at[t],
-                                            recv_sem=a_recv.at[me], device_id=(t // 2, t % 2), device_id_type=MESH)
-
-    pl.when(a + 1 < line)(lambda: up(a, True).start())
-    pl.when(a > 0)(lambda: down(a, True).start())
-    to_x(a, True).start()
-    to_y(a, True).start()
-    sibling(a, q, True).start()
 
     def along(ak, below):
         arrive(ak, q)
@@ -206,24 +214,25 @@
     n, line = bands * 2, bands // LINE
     D = node.shape[1]
     slots, peers = sel.shape
-    V, H = pl.BlockSpec(memory_space=pltpu.VMEM), pl.BlockSpec(memory_space=pl.ANY)
+    H = pl.BlockSpec(memory_space=pl.ANY)
+    inputs = (w1, w2, nw1, nw2, sel, *vecs)
     sds, sem, vm = jax.ShapeDtypeStruct, pltpu.SemaphoreType.DMA, pltpu.VMEM
     msgs = (peers, 2 * slots, D // 2)
     return pl.pallas_call(
         functools.partial(gather_kernel, bands, parts),
         out_shape=[sds((n, rows, 128), BF), sds(msgs, BF)],
-        in_specs=[V] * 5 + [H] + [V] * 6, out_specs=[H, H],
+        in_specs=[H] * 12, out_specs=[H, H],
         scratch_shapes=[
             vm((rows, 128), BF), vm(node.shape, BF), vm((16, 128), F32), vm(msgs, BF),
             sem((n,)), sem((2, line)), sem((2, line)), sem((2, line)), sem((2, line)), sem((bands,)),
-            sem((n,)), sem((n,)), sem((3,))],
+            sem((n,)), sem((n,)), sem((3,)), sem((11,)), *[vm(m.shape, m.dtype) for m in inputs]],
         compiler_params=pltpu.CompilerParams(collective_id=0, has_side_effects=True, vmem_limit_bytes=63 * 2**20),
         name="gather_weights",
-    )(w1, w2, nw1, nw2, sel, node, *vecs)
+    )(*inputs, node)
 
 
 def reduce_kernel(bands, p_ref, msg_ref, red_ref, arr_ref, own, sib, xa, yb, ya, xb, zin,
-                  own_sem, sib_recv, x1, y1, y2, x2, z_recv, send, a_recv, a_send):
+                  own_sem, sib_recv, x1, y1, y2, x2, z_recv, send, a_recv, a_send, kept_sem):
     pos = Place(bands)
     me, c, a, q = pos.me, pos.c, pos.a, pos.q
     rows = own.shape[1]
@@ -245,12 +254,15 @@
 
     order = [pos.other_a(k) for k in range(1, pos.quads)] + [a]
     square = [pl.ds(ak * LINE, LINE) for ak in order]
+    met_all = greet_all(pos)
+    kept = pltpu.make_async_copy(msg_ref.at[me], arr_ref.at[me], kept_sem)
     mine = []
     for ak, sq in zip(order, square):
         cp = pltpu.make_async_copy(p_ref.at[c, sq], own.at[sq], own_sem.at[ak])
         cp.start()
         mine.append(cp)
-    greet_all(pos)()
+    kept.start()
+    met_all()
     for ak, sq in zip(order, square):
         push(p_ref.at[1 - c, sq], sib.at[sq], sib_recv.at[ak], pos.dev(a, q, 1 - c))
 
@@ -262,7 +274,6 @@
     def _(k):
         exchange((me + k) % pos.devices).start()
 
-    arr_ref[me] = msg_ref[me]
     to_x, to_y = pos.dev(a, pos.qx, c), pos.dev(a, pos.qy, c)
 
     def add(ref, idx, other):
@@ -328,6 +339,7 @@
         pltpu.make_async_remote_copy(src_ref=msg_ref.at[t], dst_ref=arr_ref.at[t], send_sem=a_send.at[t],
                                      recv_sem=a_recv.at[t], device_id=(t // 2, t % 2), device_id_type=MESH).wait()
 
+    kept.wait()
     for cp in started:
         cp.wait_send()
 
@@ -343,14 +355,14 @@
     return pl.pallas_call(
         functools.partial(reduce_kernel, bands),
         out_shape=[sds((rows, 128), F32), sds(msgs.shape, BF)],
-        in_specs=[pl.BlockSpec(memory_space=pl.ANY), V], out_specs=[V, V],
+        in_specs=[pl.BlockSpec(memory_space=pl.ANY)] * 2, out_specs=[V, V],
         scratch_shapes=[
             pltpu.VMEM((bands, rows, 128), BF), pltpu.VMEM((bands, rows, 128), BF),
             pltpu.VMEM((quads, 2, cut, 128), BF), pltpu.VMEM((quads, 2, rows - cut, 128), BF),
             pltpu.VMEM((quads, cut, 128), BF), pltpu.VMEM((quads, rows - cut, 128), BF),
             pltpu.VMEM((quads, rows, 128), BF),
             sem((quads,)), sem((quads,)), sem((quads, 2)), sem((quads, 2)), sem((quads,)), sem((quads,)), sem((quads,)),
-            sem((8 * quads,)), sem((n,)), sem((n,))],
+            sem((8 * quads,)), sem((n,)), sem((n,)), sem],
         compiler_params=pltpu.CompilerParams(collective_id=1, has_side_effects=True, vmem_limit_bytes=63 * 2**20),
         name="reduce_grads",
     )(packed, msgs)
@@ -443,6 +455,9 @@
     weights, refs = ((), refs) if fast else (refs[:6], refs[6:])
     nout_ref, eout_ref, ngrad_ref, egrad_ref, msg_ref, *refs = refs
     outs, refs = (refs[:1], refs[1:]) if fast else (refs[:5], refs[5:])
+    if fast:
+        pack_ref, stage, refs = outs[0], refs[0], refs[1:]
+        outs = [stage]
     weights, refs = (refs[:6], refs[6:]) if fast else (weights, refs)
     w1_ref, w2_ref, nw1_ref, nw2_ref, vec_ref, snd_ref = weights
     wcat, w2h, hid_s, slope_s, nrm_s, scale_s, gath, dg, gacc, g2acc, gain_acc, shift_acc, gvec, msg_s, dpre_s, w1t, sem = refs
@@ -466,19 +481,23 @@
                 at = o + j * p + a - d * p
                 outs[0][d % 2, d // 2, at:at + b - a, :] = value[a - lo:b - lo, 128 * j:128 * j + 128].astype(BF)
 
-    def unpack():
-        stage = outs[0]
-        cp = pltpu.make_async_copy(got_ref, stage, sem)
-        cp.start()
-        cp.wait()
-
+    RANGES = (pl.ds(0, spots[2]), pl.ds(spots[2], tail - spots[2]), pl.ds(tail, 16))
+
+    def fetch(k):
+        return pltpu.make_async_copy(got_ref.at[:, :, RANGES[k]], stage.at[:, :, RANGES[k]], sem.at[k])
+
+    def deliver(k):
+        return pltpu.make_async_copy(stage.at[:, :, RANGES[k]], pack_ref.at[:, :, RANGES[k]], sem.at[k])
+
+    def unpack(mats):
         @pl.loop(0, n)
         def _(d):
-            for w_ref, p, o in zip((w1_ref, w2_ref, nw1_ref, nw2_ref), parts, spots):
+            for w_ref, p, o in mats:
                 for j in range(D // 128):
                     w_ref[pl.ds(pl.multiple_of(d * p, p), p), 128 * j:128 * j + 128] = \
                         stage[d // (n // 2), d % (n // 2), o + j * p:o + j * p + p, :]
 
+    def unpack_vectors():
         group = n // (D // 128)
         for g in range(D // 128):
             tiles = [stage[d // (n // 2), d % (n // 2), tail:tail + 16, :].astype(F32)
@@ -491,7 +510,12 @@
     @pl.when(i == 0)
     def _():
         if fast:
-            unpack()
+            for k in range(3):
+                fetch(k).start()
+            fetch(0).wait()
+            unpack(list(zip((w1_ref, w2_ref), parts, spots))[:2])
+            fetch(2).wait()
+            unpack_vectors()
         b1 = vec_ref[0:1, :].astype(F32)
         wcat[0:D, :] = w1_ref[0:D, :] * 0.5
         wcat[D:D + S, :] = (dot(snd_ref[...], w1_ref[D:2 * D, :]) * 0.5).astype(BF)
@@ -555,7 +579,7 @@
             nrm = c * s
             nrm_s[rows[r], :] = nrm.astype(BF)
             msg = nrm * gain + shift
-            eout_ref[here[r], :] = (e_ref[here[r], :].astype(F32) + jnp.where(live, msg, 0.0)).astype(BF)
+            eout_ref[here[r], :] = (e_ref[here[r], :].astype(F32) + msg).astype(BF)
             msg_s[here[r], :] = msg.astype(BF)
 
         def c1(first, last):
@@ -573,12 +597,20 @@
                 a2(t)
         c1(0, subs)
 
+    @pl.when((i < nb) & live_blk & ((blk + 1) * R > count))
+    def _():
+        live = blk * R + lax.broadcasted_iota(jnp.int32, (R, 1), 0) < count
+        eout_ref[...] = jnp.where(live, eout_ref[...].astype(F32), e_ref[...].astype(F32)).astype(BF)
+
     @pl.when((i < nb) & jnp.logical_not(live_blk))
     def _():
         eout_ref[...] = e_ref[...]
 
     @pl.when(i == nb - 1)
     def _():
+        if fast:
+            fetch(1).wait()
+            unpack(list(zip((nw1_ref, nw2_ref), parts[2:], spots[2:])))
         nb1 = vec_ref[3:4, :].astype(F32)
         ngain = vec_ref[4:5, :].astype(F32)
         nshift = vec_ref[5:6, :].astype(F32)
@@ -605,6 +637,8 @@
         gvec[3:4, :] = jnp.sum(dpre16.astype(F32), axis=0, keepdims=True)
         ngrad_ref[...] = up + dot_t(dpre16, nw1_ref[0:D, :])
         dg[...] = dot_t(dpre16, nw1_ref[D:, :]).astype(BF)
+        if fast:
+            deliver(1).start()
 
     @pl.when((i >= nb) & live_blk)
     def _():
@@ -687,8 +721,12 @@
         else:
             for d in range(n):
                 g = d * D // n // 128
-                outs[0][d % 2, d // 2, tail:tail + 16, :] = jnp.concatenate(
+                stage[d % 2, d // 2, tail:tail + 16, :] = jnp.concatenate(
                     [gvec[:, 128 * g:128 * g + 128]] * 2, axis=0).astype(BF)
+            deliver(0).start()
+            deliver(2).start()
+            for k in range(3):
+                deliver(k).wait()
 
 
 def core(bands, parts, count, sid, rid, e, cot, node, ncot, got, inc, sub=128):
@@ -714,13 +752,13 @@
         functools.partial(core_kernel, nb, R, sub, parts, fast),
         grid=(2 * nb,),
         in_specs=[pl.BlockSpec(memory_space=pltpu.SMEM), V, V, both, bb, V, V] + specs,
-        out_specs=[V, fb, V, bb] + [V] * (len(outs) - 4),
+        out_specs=[V, fb, V, bb, V] + ([H] if fast else [V] * 5),
         out_shape=outs,
-        scratch_shapes=([vm(g, BF) for g in grads[:4]] + [vm((16, D), BF), vm((S, D), BF)] if fast else []) + [
+        scratch_shapes=([vm((2, bands, rows, 128), BF)] + [vm(g, BF) for g in grads[:4]] + [vm((16, D), BF), vm((S, D), BF)] if fast else []) + [
             vm((D + S + N, D), BF), vm((D, D), BF), vm((E, D), BF), vm((E, D), BF), vm((E, D), BF),
             vm((sub, 128), F32), vm((N, D), F32), vm((N, D), BF), vm((D + S + N, D), F32), vm((D, D), F32),
             vm((8, D), F32), vm((8, D), F32), vm((8, D), F32), vm((R, D), BF), vm((R, D), BF), vm((D, D), BF),
-            pltpu.SemaphoreType.DMA],
+            pltpu.SemaphoreType.DMA((3,))],
         compiler_params=pltpu.CompilerParams(vmem_limit_bytes=63 * 2**20, dimension_semantics=("arbitrary",)),
         name="edge_node_core",
     )(count, sid.reshape(E // sub, sub), rid.reshape(E // sub, sub), e, cot, node, ncot, *weights)

time: 146 us -> 144 us (0.986)
  Pallas kernels: 145 us -> 142 us
    pallas_call x1, Pallas kernels: 68.9 us -> 39.2 us  [core(): pl.pallas_call(functools.partial(core_kernel, nb, R, sub, parts, fast), g...]
    pallas_call x1, Pallas kernels: 40.5 us -> 68.3 us  [reduce_grads(): pl.pallas_call(functools.partial(reduce_kernel, bands), out_shape=[sds((r...]
where the time goes in v5:
time: 144 us; the launch traced here: 143 us
  Pallas kernels  142 us (99%)
    pallas_call x1, Pallas kernels, reduce_grads(): pl.pallas_call(functools.partial(reduce_kernel, bands), out_shape=[sds((r...  68.3 us
    pallas_call x1, Pallas kernels, core(): pl.pallas_call(functools.partial(core_kernel, nb, R, sub, parts, fast), g...  39.2 us
    pallas_call x1, Pallas kernels, gather_weights(): pl.pallas_call(functools.partial(gather_kernel, bands, parts), out_shape=...  31.3 us
    pallas_call x1, Pallas kernels, finish(): pl.pallas_call(functools.partial(finish_kernel, bands, parts), out_shape=...  3.14 us

profile of v5, /device:TPU:0, one launch (start us, length us, event | category | flops | bytes accessed | tf_op | source)
XLA Modules:
  0.0 143.3 jit_solution(3703298051972290673)
XLA Ops:
  1.3 31.3 %gather_weights.1 = (bf16[32,464,128]{2,1,0:T(8,128)(2,1)}, bf16[32,16,256]{2,1,0:T(8,128)(2,1)}) custom-call(bf16[48,512]{1,0:T(8,128)(2,1)} %refs_0_.1, bf16[16,512]{1,0:T(8,128)(2,1)} %refs_1_.1, bf16[32,512]{1,0:T(8,128)(2,1)} %refs_2_.1, bf16[16,512]{1,0:T(8,128)(2,1)} %refs_3_.1, s32[8,32]{1,0:T(8,128)} %bitcast.9, bf16[16]{0:T(256)(128)(2,1)} %refs_5_.1, ...), custom_call_target="tpu_custom_call" | custom-call | tf_op jit(solution)/shard_map/gather_weights/pallas_call | solution.py:221
  32.6 39.2 %edge_node_core.1 = (bf16[512,512]{1,0:T(8,128)(2,1)}, bf16[8192,512]{1,0:T(8,128)(2,1)}, f32[512,512]{1,0:T(8,128)}, f32[8192,512]{1,0:T(8,128)}, bf16[32,16,25...) custom-call(s32[1]{0:T(128)S(6)} %copy.32.count_ref, s32[64,128]{1,0:T(8,128)} %bitcast.7, s32[64,128]{1,0:T(8,128)} %bitcast.8, ...), custom_call_target="tpu_custom_call" | custom-call | tf_op jit(solution)/shard_map/edge_node_core/pallas_call | solution.py:751
  71.8 68.3 %reduce_grads.1 = (f32[464,128]{1,0:T(8,128)}, bf16[32,16,256]{2,1,0:T(8,128)(2,1)}) custom-call(bf16[2,16,464,128]{3,2,1,0:T(8,128)(2,1)} %get-tuple-element.39.p_ref, bf16[32,16,256]{2,1,0:T(8,128)(2,1)} %get-tuple-element.40.msg_ref), custom_call_target="tpu_custom_call" | custom-call | tf_op jit(solution)/shard_map/reduce_grads/pallas_call | solution.py:355
  140.1 3.1 %finish.1 = (f32[512,512]{1,0:T(8,128)}, f32[48,512]{1,0:T(8,128)}, f32[16,512]{1,0:T(8,128)}, f32[32,512]{1,0:T(8,128)}, f32[16,512]{1,0:T(8,128)}, /*index=5*/...) custom-call(f32[464,128]{1,0:T(8,128)} %get-tuple-element.41.red_ref, ...), custom_call_target="tpu_custom_call" | custom-call | tf_op jit(solution)/shard_map/finish/pallas_call | solution.py:411

commit v6 on v5

--- a/solution.py
+++ b/solution.py
@@ -688,7 +688,8 @@
                 a2(t)
             if 2 <= t < subs + 2:
                 c1(t - 2)
-        g2acc[...] += t_dot(hid_s[every, :], msg_s[...])
+            if t == subs:
+                g2acc[...] += t_dot(hid_s[every, :], msg_s[...])
         sids = jnp.concatenate([v[0] for v in idx], axis=1)
         rids = jnp.concatenate([v[1] for v in idx], axis=1)
         gacc[0:D, :] += t_dot(e_ref[...], dpre_s[...])

time: 144 us -> 143 us (level)
    pallas_call x1, Pallas kernels: 68.3 us -> 51.1 us  [reduce_grads(): pl.pallas_call(functools.partial(reduce_kernel, bands), out_shape=[sds((r...]
    pallas_call x1, Pallas kernels: 39.2 us -> 55.7 us  [core(): pl.pallas_call(functools.partial(core_kernel, nb, R, sub, parts, fast), g...]
where the time goes in v6:
time: 143 us
  Pallas kernels  141 us (99%)
    pallas_call x1, Pallas kernels, core(): pl.pallas_call(functools.partial(core_kernel, nb, R, sub, parts, fast), g...  55.7 us
    pallas_call x1, Pallas kernels, reduce_grads(): pl.pallas_call(functools.partial(reduce_kernel, bands), out_shape=[sds((r...  51.1 us
    pallas_call x1, Pallas kernels, gather_weights(): pl.pallas_call(functools.partial(gather_kernel, bands, parts), out_shape=...  31.3 us
    pallas_call x1, Pallas kernels, finish(): pl.pallas_call(functools.partial(finish_kernel, bands, parts), out_shape=...  3.15 us

profile of v6, /device:TPU:0, one launch (start us, length us, event | category | flops | bytes accessed | tf_op | source)
XLA Modules:
  0.0 142.6 jit_solution(10687556568426563376)
XLA Ops:
  1.3 31.3 %gather_weights.1 = (bf16[32,464,128]{2,1,0:T(8,128)(2,1)}, bf16[32,16,256]{2,1,0:T(8,128)(2,1)}) custom-call(bf16[48,512]{1,0:T(8,128)(2,1)} %refs_0_.1, bf16[16,512]{1,0:T(8,128)(2,1)} %refs_1_.1, bf16[32,512]{1,0:T(8,128)(2,1)} %refs_2_.1, bf16[16,512]{1,0:T(8,128)(2,1)} %refs_3_.1, s32[8,32]{1,0:T(8,128)} %bitcast.9, bf16[16]{0:T(256)(128)(2,1)} %refs_5_.1, ...), custom_call_target="tpu_custom_call" | custom-call | tf_op jit(solution)/shard_map/gather_weights/pallas_call | solution.py:221
  32.6 55.7 %edge_node_core.1 = (bf16[512,512]{1,0:T(8,128)(2,1)}, bf16[8192,512]{1,0:T(8,128)(2,1)}, f32[512,512]{1,0:T(8,128)}, f32[8192,512]{1,0:T(8,128)}, bf16[32,16,25...) custom-call(s32[1]{0:T(128)S(6)} %copy.32.count_ref, s32[64,128]{1,0:T(8,128)} %bitcast.7, s32[64,128]{1,0:T(8,128)} %bitcast.8, ...), custom_call_target="tpu_custom_call" | custom-call | tf_op jit(solution)/shard_map/edge_node_core/pallas_call | solution.py:752
  88.4 51.1 %reduce_grads.1 = (f32[464,128]{1,0:T(8,128)}, bf16[32,16,256]{2,1,0:T(8,128)(2,1)}) custom-call(bf16[2,16,464,128]{3,2,1,0:T(8,128)(2,1)} %get-tuple-element.39.p_ref, bf16[32,16,256]{2,1,0:T(8,128)(2,1)} %get-tuple-element.40.msg_ref), custom_call_target="tpu_custom_call" | custom-call | tf_op jit(solution)/shard_map/reduce_grads/pallas_call | solution.py:355
  139.4 3.1 %finish.1 = (f32[512,512]{1,0:T(8,128)}, f32[48,512]{1,0:T(8,128)}, f32[16,512]{1,0:T(8,128)}, f32[32,512]{1,0:T(8,128)}, f32[16,512]{1,0:T(8,128)}, /*index=5*/...) custom-call(f32[464,128]{1,0:T(8,128)} %get-tuple-element.41.red_ref, ...), custom_call_target="tpu_custom_call" | custom-call | tf_op jit(solution)/shard_map/finish/pallas_call | solution.py:411
